TPU v7x, 256 devices: a whole 4x4x8 slice. The times are simulated.
256 devices in a mesh: row: 32 (over x_lo, z, core), col: 8 (over x_hi, y).
Axes of the slice: x: 4 (x_hi: 2, x_lo: 2; x = x_hi * 2 + x_lo), y: 4, z: 8, core: 2. Of those that a mesh axis runs over, the one named last changes fastest.
Arguments:
- embed: float32 [1024, 512], P('row', 'col'), may hold values from -6 to 6
- proj: float32 [512, 48], P('col'), may hold values from -0.25 to 0.25
- pair_in: float32 [48, 1024, 1024], P(None, 'row', 'col'), may hold values from -6 to 6
- kernels: float32 [2, 48, 48, 3, 3], replicated, may hold values from -0.3125 to 0.3125
- dilation: int32 [2], replicated, may hold values from 1 to 4, as said below
- cotangent: float32 [48, 1024, 1024], P(None, 'row', 'col'), may hold values from -0.75 to 0.75
Outputs:
- pair_out: float32 [48, 1024, 1024], P(None, 'row', 'col')
- embed_grad: float32 [1024, 512], P('row', 'col')
Inputs may be any that keep to these rules, and one draw needn't show every extreme that they name: Each dilation is 1 to 4, and one of them equals 4.
All inputs are finite; a program needn't handle non-finite values.
Results may differ from a plain program's by a relative error of at most 0.00011.
Values sent between devices are 32-bit elements; how exact they have to be, the bound alone decides.
No kernel may reach another device: no remote copies, remote signals or barrier semaphores. Data moves between devices by JAX's collectives and lax.ppermute only.
A program may use at most 64 MiB of HBM per device.

v0:
```python
import functools

import jax
import jax.numpy as jnp
from jax import lax
from jax.experimental import pallas as pl
from jax.experimental.pallas import tpu as pltpu
from jax.sharding import PartitionSpec as P

C = 48
ROWS = 32
COLS = 128
HALO = 12
GHALO = 4
EXT = ROWS + 2 * HALO
GEXT = ROWS + 2 * GHALO
TAPS = 9 * C
BINS = 1024
PEERS = 16
F32 = jnp.float32
BF16 = jnp.bfloat16
VMEM = pl.BlockSpec(memory_space=pltpu.VMEM)
SMEM = pl.BlockSpec(memory_space=pltpu.SMEM)
PARAMS = pltpu.CompilerParams(vmem_limit_bytes=56 * 2**20)


def lanes_of(rows, width=COLS):
    return lax.broadcasted_iota(jnp.int32, (rows, width), 1)


def turn(value, shift):
    width = value.shape[-1]
    if isinstance(shift, int):
        shift = shift % width
        if shift == 0:
            return value
    return pltpu.roll(value, shift, value.ndim - 1)


def spread(first, second):
    low = lanes_of(C // 2) < 64
    top = jnp.where(low, first, turn(second, 64))
    bottom = jnp.where(low, turn(first, 64), second)
    return jnp.concatenate([top, bottom], axis=0)


def packed(value):
    low = lanes_of(C // 2) < 64
    top, bottom = value[: C // 2], value[C // 2 :]
    first = jnp.where(low, top, turn(bottom, 64))
    second = jnp.where(low, turn(top, 64), bottom)
    return first, second


def project_kernel(scal, embed, proj, out):
    core = scal[2] % 2
    part = lax.dot_general(
        proj[...].T, embed[...].T, (((1,), (0,)), ((), ())),
        precision=lax.Precision.HIGHEST, preferred_element_type=F32,
    )
    part = jnp.concatenate([part, jnp.zeros((C, COLS - ROWS), F32)], axis=1)
    mine = turn(part[: C // 2], 32 * core) + turn(part[C // 2 :], 64 + 32 * core)
    for peer in range(PEERS):
        out[peer] = mine


def strips_kernel(pair, cot, above, below, xm, gm, to_left, to_right):
    for e in range(HALO):
        xm[e] = above[pl.ds(e, C, stride=16), :]
        xm[e + HALO + ROWS] = below[pl.ds(e, C, stride=16), :]
    for e in range(GHALO):
        gm[e] = above[pl.ds(e + HALO, C, stride=16), :]
        gm[e + GHALO + ROWS] = below[pl.ds(e + HALO, C, stride=16), :]
    for i in range(ROWS):
        xm[i + HALO] = pair[pl.ds(i, C, stride=ROWS), :]
        gm[i + GHALO] = cot[pl.ds(i, C, stride=ROWS), :]
    lane = lanes_of(C)

    def body(k, carry):
        g_first = jnp.clip(k - 1, 0, 4) * 8
        left = jnp.zeros((C, COLS), F32)
        right = jnp.zeros((C, COLS), F32)
        for s in range(8):
            x = xm[8 * k + s]
            g = gm[g_first + s]
            slot = (lane >= 16 * s) & (lane < 16 * s + 16)
            to_l = jnp.where(lane < 12, x, turn(g, 12))
            to_r = jnp.where(lane < 116, turn(g, -12), x)
            left = jnp.where(slot, turn(to_l, 16 * s), left)
            right = jnp.where(slot, turn(to_r, 16 * s - 112), right)
        to_left[k] = left
        to_right[k] = right
        return carry

    lax.fori_loop(0, EXT // 8, body, 0)


def dot(a, b):
    return jnp.dot(a, b, preferred_element_type=F32)


def split(value):
    hi = value.astype(BF16)
    lo = (value - hi.astype(F32)).astype(BF16)
    return hi, lo


def weighted(weights, x_hi, x_lo):
    both = dot(weights, x_hi)
    low = dot(weights[:C], x_lo)
    return both[:C] + (both[C:] + low)


def main_kernel(
    scal, xm, gm, from_left, from_right, fields, mats, pair_out, send,
    x0, xh, xl, yh, yl, sh, sl, gb, t0s, s0s, g1s, wts, buf,
):
    d0, d1, row, col = scal[0], scal[1], scal[2], scal[3]
    lane = lanes_of(C)
    for m in range(4):
        hi, lo = split(mats[m])
        wts[m, :C] = hi
        wts[m, C:] = lo
    own_u = spread(fields[2 * col], fields[2 * col + 1])
    side_u = spread(fields[jnp.minimum(2 * col + 2, PEERS - 1)], fields[jnp.maximum(2 * col - 1, 0)])
    group, core = row // 2, row % 2
    near = jnp.clip(group - 1 + core, 0, PEERS - 1)
    far = jnp.clip(group + core, 0, PEERS - 1)
    row_u = turn(spread(fields[near], fields[far]), 76 + 32 * core)
    inside = ((lane < HALO) & (col < 7)) | ((lane >= COLS - HALO) & (col > 0))
    side_mask = jnp.where(inside, 1.0, 0.0).astype(F32)
    full_mask = jnp.concatenate([jnp.ones((C, COLS), F32), side_mask], axis=1)
    side_u = side_u * side_mask

    def row_mask(e):
        at = row * ROWS + e - HALO
        return jnp.where((at >= 0) & (at < BINS), 1.0, 0.0).astype(F32)

    def put_shifted(hi_ref, lo_ref, e, value, step, width):
        n = value.shape[-1]
        for b, shift in enumerate((n - step, 0, step)):
            moved = value if b == 1 else turn(value, shift)
            hi, lo = split(moved[:, :width])
            hi_ref[e, b * C : (b + 1) * C] = hi
            lo_ref[e, b * C : (b + 1) * C] = lo

    def assemble(k, carry):
        ur = turn(row_u, (COLS - 8 * k) % COLS)
        fl = from_left[k]
        fr = from_right[k]
        for s in range(8):
            e = 8 * k + s
            keep = row_mask(e)
            ui = jnp.broadcast_to(ur[:, s : s + 1], (C, COLS)) * keep
            main = xm[e] + (ui + own_u * keep)
            side = jnp.where(
                lane < HALO, turn(fr, -16 * s),
                jnp.where(lane >= COLS - HALO, turn(fl, 112 - 16 * s), 0.0),
            )
            side = side + (ui * side_mask + side_u * keep)
            whole = jnp.concatenate([main, side], axis=1)
            x0[e] = whole
            put_shifted(xh, xl, e, whole, -d0 % 256, 2 * COLS)
        return carry

    lax.fori_loop(0, EXT // 8, assemble, 0)

    def assemble_g(k, carry):
        fl = from_left[k + 1]
        fr = from_right[k + 1]
        for s in range(8):
            gb[8 * k + s] = jnp.where(
                lane < GHALO, turn(fr, -(16 * s + 12)),
                jnp.where(lane >= COLS - GHALO, turn(fl, 124 - 16 * s), 0.0),
            )
        return carry

    lax.fori_loop(0, GEXT // 8, assemble_g, 0)

    def stacked(ref, lowest, middle, highest):
        return jnp.concatenate([ref[lowest], ref[middle], ref[highest]], axis=0)

    def first(i, carry):
        e = i + 4
        acc = weighted(
            wts[0], stacked(xh, e - d0, e, e + d0), stacked(xl, e - d0, e, e + d0)
        )
        t = jnp.tanh(acc)
        t0s[e] = t[:, :COLS]
        h = x0[e] + t * (full_mask * row_mask(e))
        x0[e] = h
        put_shifted(yh, yl, e, h, -d1 % 256, 2 * COLS)
        return carry

    lax.fori_loop(0, EXT - 8, first, 0, unroll=4)

    def second(e, own):
        acc = weighted(
            wts[1], stacked(yh, e - d1, e, e + d1), stacked(yl, e - d1, e, e + d1)
        )
        t = jnp.tanh(acc)
        if own:
            pair_out[pl.ds(e - HALO, C, stride=ROWS), :] = x0[e, :, :COLS] + t[:, :COLS]
        g = jnp.concatenate([gm[e - 8], gb[e - 8]], axis=1)
        scaled = g * (1.0 - t * t)
        put_shifted(sh, sl, e - 8, scaled, d1, COLS)

    def second_own(i, carry):
        second(i + HALO, True)
        return carry

    for e in (8, 9, 10, 11, 44, 45, 46, 47):
        second(e, False)
    lax.fori_loop(0, ROWS, second_own, 0, unroll=4)

    def third(i, carry):
        parts_hi, parts_lo = [], []
        for k in range(2):
            q = 2 * i + k + GHALO
            parts_hi.append(stacked(sh, q + d1, q, q - d1))
            parts_lo.append(stacked(sl, q + d1, q, q - d1))
        acc = weighted(
            wts[2], jnp.concatenate(parts_hi, axis=1), jnp.concatenate(parts_lo, axis=1)
        )
        for k in range(2):
            at = 2 * i + k
            g1 = gm[at + GHALO] + acc[:, k * COLS : (k + 1) * COLS]
            t = t0s[at + HALO]
            g1s[at] = g1
            s0s[at] = g1 * (1.0 - t * t)
        return carry

    lax.fori_loop(0, ROWS // 2, third, 0, unroll=4)

    at_col = col * COLS + lane
    keep_up = jnp.where(at_col < BINS - d0, 1.0, 0.0).astype(F32)
    keep_down = jnp.where(at_col >= d0, 1.0, 0.0).astype(F32)
    zero = jnp.zeros((C, COLS), F32)

    def sums(i, carry):
        s0, g1 = s0s[i], g1s[i]
        at = row * ROWS + i
        up = jnp.where(at < BINS - d0, 1.0, 0.0).astype(F32)
        down = jnp.where(at >= d0, 1.0, 0.0).astype(F32)
        cg, cd, c0, cu, rg, rd, r0, ru = carry
        here = lane == i

        def place(total, value):
            return jnp.where(here, jnp.sum(value, axis=1, keepdims=True), total)

        return (
            cg + g1, cd + s0 * down, c0 + s0, cu + s0 * up,
            place(rg, g1), place(rd, s0 * keep_down), place(r0, s0), place(ru, s0 * keep_up),
        )

    cg, cd, c0, cu, rg, rd, r0, ru = lax.fori_loop(0, ROWS, sums, (zero,) * 8)
    blocks = []
    for part in (cd, c0, cu):
        wide = jnp.concatenate([part, zero], axis=1)
        blocks += [turn(wide, 256 - d0), wide, turn(wide, d0)]
    col_x = jnp.concatenate(blocks, axis=0)
    blocks = []
    for a in range(3):
        for part in (rd, r0, ru):
            blocks.append((turn(part, COLS - d0), part, turn(part, d0))[a])
    row_x = jnp.concatenate(blocks, axis=0)
    hi, lo = split(jnp.concatenate([col_x, row_x], axis=1))
    made = weighted(wts[3], hi, lo)
    buf[...] = jnp.zeros(buf.shape, F32)

    def add(first_at, second_at, value):
        one, two = packed(value)
        buf[first_at] = buf[first_at] + one
        buf[second_at] = buf[second_at] + two

    add(2 * col + 1, 2 * col + 2, cg + made[:, :COLS])
    add(2 * col + 3, 2 * col, made[:, COLS : 2 * COLS])
    add(group + core, group + core + 1, turn(rg + made[:, 2 * COLS :], 64 - 32 * core))
    send[...] = buf[1 : PEERS + 1]


def finish_kernel(scal, parts, proj, out):
    core = scal[2] % 2
    total = parts[0]
    for peer in range(1, PEERS):
        total = total + parts[peer]
    both = jnp.concatenate([turn(total, 128 - 32 * core), turn(total, 64 - 32 * core)], axis=0)
    grad = lax.dot_general(
        proj[...], both, (((1,), (0,)), ((), ())),
        precision=lax.Precision.HIGHEST, preferred_element_type=F32,
    )
    out[...] = grad.T[:ROWS]


def local(embed, proj, pair_in, kernels, dilation, cotangent):
    rows, cols = 32, 8
    row = lax.axis_index("row")
    col = lax.axis_index("col")
    scal = jnp.stack([dilation[0], dilation[1], row, col]).astype(jnp.int32)
    down = [(i, i + 1) for i in range(rows - 1)]
    up = [(i + 1, i) for i in range(rows - 1)]
    right = [(i, i + 1) for i in range(cols - 1)]
    left = [(i + 1, i) for i in range(cols - 1)]
    same_core = [[2 * i + core for i in range(PEERS)] for core in range(2)]
    chips = [[(2 * g + core) * cols + c for core in range(2) for c in range(cols)] for g in range(PEERS)]

    low_edge = jnp.concatenate([pair_in[:, ROWS - HALO :], cotangent[:, ROWS - GHALO :]], axis=1)
    high_edge = jnp.concatenate([pair_in[:, :HALO], cotangent[:, :GHALO]], axis=1)
    above = lax.ppermute(low_edge, "row", down)
    below = lax.ppermute(high_edge, "row", up)

    packs = jax.ShapeDtypeStruct((PEERS, C // 2, COLS), F32)
    parts = pl.pallas_call(
        project_kernel, in_specs=[SMEM, VMEM, VMEM], out_specs=VMEM, out_shape=packs, name="project",
    )(scal, embed, proj)
    parts = lax.all_to_all(parts, ("row", "col"), 0, 0, tiled=True, axis_index_groups=chips)

    xm, gm, to_left, to_right = pl.pallas_call(
        strips_kernel,
        in_specs=[VMEM] * 4,
        out_specs=[VMEM] * 4,
        out_shape=[
            jax.ShapeDtypeStruct((EXT, C, COLS), F32),
            jax.ShapeDtypeStruct((GEXT, C, COLS), F32),
            jax.ShapeDtypeStruct((EXT // 8, C, COLS), F32),
            jax.ShapeDtypeStruct((EXT // 8, C, COLS), F32),
        ],
        compiler_params=PARAMS,
        name="strips",
    )(
        pair_in.reshape(C * ROWS, COLS), cotangent.reshape(C * ROWS, COLS),
        above.reshape(C * 16, COLS), below.reshape(C * 16, COLS),
    )
    from_left = lax.ppermute(to_right, "col", right)
    from_right = lax.ppermute(to_left, "col", left)

    own = jnp.sum(parts, axis=0)
    fields = lax.all_to_all(
        jnp.broadcast_to(own, (PEERS,) + own.shape), "row", 0, 0, tiled=True, axis_index_groups=same_core
    )

    forward = kernels.transpose(0, 1, 3, 4, 2).reshape(2, C, TAPS)
    backward = kernels.transpose(0, 2, 3, 4, 1).reshape(2, C, TAPS)
    mats = jnp.stack([forward[0], forward[1], backward[1], backward[0]])
    pair_out, send = pl.pallas_call(
        main_kernel,
        in_specs=[SMEM] + [VMEM] * 6,
        out_specs=[VMEM] * 2,
        out_shape=[jax.ShapeDtypeStruct((C * ROWS, COLS), F32), packs],
        scratch_shapes=[
            pltpu.VMEM((EXT, C, 2 * COLS), F32),
            pltpu.VMEM((EXT, 3 * C, 2 * COLS), BF16),
            pltpu.VMEM((EXT, 3 * C, 2 * COLS), BF16),
            pltpu.VMEM((EXT, 3 * C, 2 * COLS), BF16),
            pltpu.VMEM((EXT, 3 * C, 2 * COLS), BF16),
            pltpu.VMEM((GEXT, 3 * C, COLS), BF16),
            pltpu.VMEM((GEXT, 3 * C, COLS), BF16),
            pltpu.VMEM((GEXT, C, COLS), F32),
            pltpu.VMEM((EXT, C, COLS), F32),
            pltpu.VMEM((ROWS, C, COLS), F32),
            pltpu.VMEM((ROWS, C, COLS), F32),
            pltpu.VMEM((4, 2 * C, TAPS), BF16),
            pltpu.VMEM((PEERS + 2, C // 2, COLS), F32),
        ],
        compiler_params=PARAMS,
        name="layers",
    )(scal, xm, gm, from_left, from_right, fields, mats)

    got = lax.all_to_all(send, "row", 0, 0, tiled=True, axis_index_groups=same_core)
    own = jnp.sum(got, axis=0)
    got = lax.all_to_all(
        jnp.broadcast_to(own, (PEERS,) + own.shape), ("row", "col"), 0, 0, tiled=True, axis_index_groups=chips
    )
    embed_grad = pl.pallas_call(
        finish_kernel, in_specs=[SMEM, VMEM, VMEM], out_specs=VMEM,
        out_shape=jax.ShapeDtypeStruct((ROWS, 64), F32), name="finish",
    )(scal, got, proj)
    return (pair_out.reshape(C, ROWS, COLS), embed_grad)


def solution(mesh):
    in_specs = (
        P("row", "col"),
        P("col", None),
        P(None, "row", "col"),
        P(),
        P(),
        P(None, "row", "col"),
    )
    out_specs = (P(None, "row", "col"), P("row", "col"))
    return jax.shard_map(local, mesh=mesh, in_specs=in_specs, out_specs=out_specs, check_vma=False)
```

profile of v0, /device:TPU:1, one launch (start us, length us, event | category | flops | bytes accessed | tf_op | source)
XLA Modules:
  0.0 113.5 jit_solution(832150768211754975)
XLA Ops:
  0.6 0.0 copy-start
  0.6 1.5 %copy.14.proj = f32[64,48]{1,0:T(8,128)} copy(f32[64,48]{0,1:T(8,128)} %param.7) | data formatting | bytes 24576 | tf_op args[1]
  2.1 1.3 %pad_add_fusion.scal = s32[4]{0:T(128)} fusion(s32[1]{0:T(128)} %bitcast.1, s32[1]{0:T(128)} %bitcast, s32[2]{0:T(128)} %param.10), kind=kLoop, calls=%fused_computation.3 | loop fusion | flops 8 | bytes 32 | tf_op jit(solution)/shard_map/stack | solution.py:299
  3.4 1.8 %project.1 = f32[16,24,128]{2,1,0:T(8,128)} custom-call(s32[4]{0:T(128)} %pad_add_fusion.scal, f32[32,64]{1,0:T(8,128)} %embed.1, f32[64,48]{1,0:T(8,128)} %copy.14.proj), custom_call_target="tpu_custom_call" | custom-call | tf_op jit(solution)/shard_map/project/pallas_call | solution.py:313
  5.2 8.5 %all-to-all-start = ((f32[16,24,128]{2,1,0:T(8,128)}), f32[16,24,128]{2,1,0:T(8,128)S(1)}, u32[]{:S(2)}, u32[]{:S(2)}) async-start(f32[16,24,128]{2,1,0:T(8,128)} %project.1), calls=%async_computation | async-start | bytes 393216 | tf_op jit(solution)/shard_map/all_to_all | solution.py:316
  13.6 1.1 fusion.1
  14.7 0.0 copy-done
  14.7 0.1 fusion
  14.8 0.0 copy-start.1
  14.8 0.1 pad_maximum_fusion
  14.9 3.7 %collective-permute-start = (f32[48,16,128]{2,1,0:T(8,128)S(1)}, f32[48,16,128]{2,1,0:T(8,128)S(1)}, u32[]{:S(2)}, u32[]{:S(2)}) collective-permute-start(f32[48,16,128]{2,1,0:T(8,128)S(1)} %pad_maximum_fusion), channel_id=1, source_target_pairs={{0,8},{8,16},{16,24},{24,32},{32,40},{40,48},{48,56},{56,64},{64,7... | collective-permute-start | bytes 1179656 | tf_op jit(solution)/shard_map/ppermute | solution.py:309
  18.5 0.1 pad_maximum_fusion.1
  18.6 1.9 %collective-permute-start.1 = (f32[48,16,128]{2,1,0:T(8,128)S(1)}, f32[48,16,128]{2,1,0:T(8,128)S(1)}, u32[]{:S(2)}, u32[]{:S(2)}) collective-permute-start(f32[48,16,128]{2,1,0:T(8,128)S(1)} %pad_maximum_fusion.1), channel_id=1, source_target_pairs={{8,0},{16,8},{24,16},{32,24},{40,32},{48,40},{56,48},{64,56},{72,6... | collective-permute-start | bytes 1179656 | tf_op jit(solution)/shard_map/ppermute | solution.py:310
  20.5 1.7 %all-to-all-done = f32[16,24,128]{2,1,0:T(8,128)S(1)} async-done(((f32[16,24,128]{2,1,0:T(8,128)}), f32[16,24,128]{2,1,0:T(8,128)S(1)}, u32[]{:S(2)}, u32[]{:S(2)}) %all-to-all-start) | async-done | bytes 196640 | tf_op jit(solution)/shard_map/all_to_all | solution.py:316
  22.2 0.7 broadcast_in_dim.6
  22.9 8.3 %all-to-all-start.1 = ((f32[16,24,128]{2,1,0:T(8,128)}), f32[16,24,128]{2,1,0:T(8,128)S(1)}, u32[]{:S(2)}, u32[]{:S(2)}) async-start(f32[16,24,128]{2,1,0:T(8,128)} %broadcast_in_dim.6), calls=%async_computation.1 | async-start | bytes 393216 | tf_op jit(solution)/shard_map/all_to_all | solution.py:338
  31.2 0.0 copy-done.1
  31.3 0.0 collective-permute-done
  31.3 0.0 copy-start.3
  31.3 0.0 collective-permute-done.1
  31.3 0.0 copy-start.4
  31.3 0.7 copy-done.3
  32.1 0.1 copy-done.4
  32.2 7.1 %strips.1 = (f32[56,48,128]{2,1,0:T(8,128)}, f32[40,48,128]{2,1,0:T(8,128)}, f32[7,48,128]{2,1,0:T(8,128)}, f32[7,48,128]{2,1,0:T(8,128)}) custom-call(f32[1536,128]{1,0:T(8,128)} %bitcast.11, f32[1536,128]{1,0:T(8,128)} %bitcast.14, f32[768,128]{1,0:T(8,128)} %bitcast.17, f32[768,128]{1,0:T(8,128)} %bitcast.18), custom_call_target="tpu_custom_call" | custom-call | tf_op jit(solution)/shard_map/strips/pallas_call | solution.py:318
  39.2 2.2 %collective-permute-start.2 = (f32[7,48,128]{2,1,0:T(8,128)}, f32[7,48,128]{2,1,0:T(8,128)S(1)}, u32[]{:S(2)}, u32[]{:S(2)}) collective-permute-start(f32[7,48,128]{2,1,0:T(8,128)} %get-tuple-element.10), channel_id=1, source_target_pairs={{0,1},{1,2},{2,3},{3,4},{4,5},{5,6},{6,7},{8,9},{9,10},{10,11},{11... | collective-permute-start | bytes 516104 | tf_op jit(solution)/shard_map/ppermute | solution.py:334
  41.4 1.3 %collective-permute-start.3 = (f32[7,48,128]{2,1,0:T(8,128)}, f32[7,48,128]{2,1,0:T(8,128)S(1)}, u32[]{:S(2)}, u32[]{:S(2)}) collective-permute-start(f32[7,48,128]{2,1,0:T(8,128)} %get-tuple-element.11), channel_id=1, source_target_pairs={{1,0},{2,1},{3,2},{4,3},{5,4},{6,5},{7,6},{9,8},{10,9},{11,10},{12... | collective-permute-start | bytes 516104 | tf_op jit(solution)/shard_map/ppermute | solution.py:335
  42.8 0.1 copy.15
  42.9 0.2 slice.44
  43.1 0.1 copy.16
  43.2 0.2 slice.46
  43.4 0.1 copy.20
  43.5 0.1 copy.21
  43.6 0.8 pad_maximum_fusion.2.mats
  44.4 0.0 all-to-all-done.1.fields
  44.4 0.0 copy-start.2
  44.4 0.0 collective-permute-done.2.from_left
  44.4 0.0 copy-start.5
  44.4 3.4 %collective-permute-done.3.from_right = f32[7,48,128]{2,1,0:T(8,128)S(1)} collective-permute-done((f32[7,48,128]{2,1,0:T(8,128)}, f32[7,48,128]{2,1,0:T(8,128)S(1)}, u32[]{:S(2)}, u32[]{:S(2)}) %collective-permute-start.3) | collective-permute-done | bytes 172064 | tf_op jit(solution)/shard_map/ppermute | solution.py:335
  47.8 0.0 copy-start.6
  47.8 0.0 copy-done.2
  47.8 0.0 copy-done.5
  47.8 0.7 copy-done.6
  48.5 26.0 %layers.1 = (f32[1536,128]{1,0:T(8,128)}, f32[16,24,128]{2,1,0:T(8,128)}) custom-call(s32[4]{0:T(128)} %pad_add_fusion.scal, f32[56,48,128]{2,1,0:T(8,128)} %get-tuple-element.8.xm, f32[40,48,128]{2,1,0:T(8,128)} %get-tuple-element.9.gm, f32[7,48,128]{2,1,0:T(8,128)} %copy-done.5, f32[7,48,128]{2,1,0:T(8,128)} %copy-done.6, f32[16,24,128]{2,1,0:T(8,128)} %copy-done.2, ...), custom_call_target="tpu_custom_call" | custom-call | tf_op jit(solution)/shard_map/layers/pallas_call | solution.py:345
  74.5 15.0 %all_to_all.20 = f32[16,24,128]{2,1,0:T(8,128)S(1)} all-to-all(f32[16,24,128]{2,1,0:T(8,128)} %get-tuple-element.13), channel_id=1, replica_groups={{0,16,32,48,64,80,96,112,128,144,160,176,192,208,224,240},{8,24,40,56,7..., dimensions={0} | all-to-all | bytes 393216 | tf_op jit(solution)/shard_map/all_to_all | solution.py:369
  89.5 22.1 %all_to_all.21.parts = f32[16,24,128]{2,1,0:T(8,128)} all-to-all(f32[16,24,128]{2,1,0:T(8,128)S(1)} %broadcast_in_dim.7), channel_id=1, replica_groups={{0,1,2,3,4,5,6,7,8,9,10,11,12,13,14,15},{16,17,18,19,20,21,22,23,24,25,..., dimensions={0} | all-to-all | bytes 393216 | tf_op jit(solution)/shard_map/all_to_all | solution.py:371
  111.6 1.9 %finish.1 = f32[32,64]{1,0:T(8,128)} custom-call(s32[4]{0:T(128)} %pad_add_fusion.scal, f32[16,24,128]{2,1,0:T(8,128)} %all_to_all.21.parts, f32[64,48]{1,0:T(8,128)} %copy.14.proj), custom_call_target="tpu_custom_call" | custom-call | tf_op jit(solution)/shard_map/finish/pallas_call | solution.py:374
  (5 shorter events, 0.1 us)
Async XLA Ops:
  0.6 14.1 %copy-start = (f32[48,32,128]{2,1,0:T(8,128)S(1)}, f32[48,32,128]{2,1,0:T(8,128)}, u32[]{:S(2)}) copy-start(f32[48,32,128]{2,1,0:T(8,128)} %param.8) | copy-start | bytes 2359300
  5.2 17.0 %all-to-all-start = ((f32[16,24,128]{2,1,0:T(8,128)}), f32[16,24,128]{2,1,0:T(8,128)S(1)}, u32[]{:S(2)}, u32[]{:S(2)}) async-start(f32[16,24,128]{2,1,0:T(8,128)} %project.1), calls=%async_computation | async-start | bytes 393216 | tf_op jit(solution)/shard_map/all_to_all | solution.py:316
  14.8 16.5 %copy-start.1 = (f32[2,48,48,3,3]{2,1,4,3,0:T(8,128)S(1)}, f32[2,48,48,3,3]{2,1,4,3,0:T(8,128)}, u32[]{:S(2)}) copy-start(f32[2,48,48,3,3]{2,1,4,3,0:T(8,128)} %param.9) | copy-start | bytes 497668
  14.9 16.4 %collective-permute-start = (f32[48,16,128]{2,1,0:T(8,128)S(1)}, f32[48,16,128]{2,1,0:T(8,128)S(1)}, u32[]{:S(2)}, u32[]{:S(2)}) collective-permute-start(f32[48,16,128]{2,1,0:T(8,128)S(1)} %pad_maximum_fusion), channel_id=1, source_target_pairs={{0,8},{8,16},{16,24},{24,32},{32,40},{40,48},{48,56},{56,64},{64,7... | collective-permute-start | bytes 1179656 | tf_op jit(solution)/shard_map/ppermute | solution.py:309
  18.6 12.7 %collective-permute-start.1 = (f32[48,16,128]{2,1,0:T(8,128)S(1)}, f32[48,16,128]{2,1,0:T(8,128)S(1)}, u32[]{:S(2)}, u32[]{:S(2)}) collective-permute-start(f32[48,16,128]{2,1,0:T(8,128)S(1)} %pad_maximum_fusion.1), channel_id=1, source_target_pairs={{8,0},{16,8},{24,16},{32,24},{40,32},{48,40},{56,48},{64,56},{72,6... | collective-permute-start | bytes 1179656 | tf_op jit(solution)/shard_map/ppermute | solution.py:310
  22.9 21.4 %all-to-all-start.1 = ((f32[16,24,128]{2,1,0:T(8,128)}), f32[16,24,128]{2,1,0:T(8,128)S(1)}, u32[]{:S(2)}, u32[]{:S(2)}) async-start(f32[16,24,128]{2,1,0:T(8,128)} %broadcast_in_dim.6), calls=%async_computation.1 | async-start | bytes 393216 | tf_op jit(solution)/shard_map/all_to_all | solution.py:338
  31.3 0.7 copy-start.3
  31.3 0.9 copy-start.4
  39.2 5.1 %collective-permute-start.2 = (f32[7,48,128]{2,1,0:T(8,128)}, f32[7,48,128]{2,1,0:T(8,128)S(1)}, u32[]{:S(2)}, u32[]{:S(2)}) collective-permute-start(f32[7,48,128]{2,1,0:T(8,128)} %get-tuple-element.10), channel_id=1, source_target_pairs={{0,1},{1,2},{2,3},{3,4},{4,5},{5,6},{6,7},{8,9},{9,10},{10,11},{11... | collective-permute-start | bytes 516104 | tf_op jit(solution)/shard_map/ppermute | solution.py:334
  41.4 6.4 %collective-permute-start.3 = (f32[7,48,128]{2,1,0:T(8,128)}, f32[7,48,128]{2,1,0:T(8,128)S(1)}, u32[]{:S(2)}, u32[]{:S(2)}) collective-permute-start(f32[7,48,128]{2,1,0:T(8,128)} %get-tuple-element.11), channel_id=1, source_target_pairs={{1,0},{2,1},{3,2},{4,3},{5,4},{6,5},{7,6},{9,8},{10,9},{11,10},{12... | collective-permute-start | bytes 516104 | tf_op jit(solution)/shard_map/ppermute | solution.py:335
  44.4 3.4 %copy-start.2 = (f32[16,24,128]{2,1,0:T(8,128)}, f32[16,24,128]{2,1,0:T(8,128)S(1)}, u32[]{:S(2)}) copy-start(f32[16,24,128]{2,1,0:T(8,128)S(1)} %all-to-all-done.1.fields) | copy-start | bytes 589828
  44.4 3.4 %copy-start.5 = (f32[7,48,128]{2,1,0:T(8,128)}, f32[7,48,128]{2,1,0:T(8,128)S(1)}, u32[]{:S(2)}) copy-start(f32[7,48,128]{2,1,0:T(8,128)S(1)} %collective-permute-done.2.from_left) | copy-start | bytes 516100
  47.8 0.7 copy-start.6
where the time goes:
time: 114 us; the launch traced here: 113 us
  blocking collectives  37.1 us (33%)
  Pallas kernels  36.7 us (32%)
  starting transfers between devices  25.8 us (23%)
  local copies, waits for them, and re-layouts  5.72 us (5%)
  waiting for transfers between devices  5.09 us (4%)
  other arithmetic  2.23 us (2%)
    pallas_call x1, Pallas kernels, local(): pl.pallas_call(main_kernel, in_specs=[SMEM] + [VMEM] * 6, out_specs=[VMEM...  26 us
    all_to_all x1, blocking collectives, local(): lax.all_to_all(jnp.broadcast_to(own, (PEERS,) + own.shape), ('row', 'col'...  22.1 us
    all_to_all x1, blocking collectives, local(): lax.all_to_all(send, 'row', 0, 0, tiled=True, axis_index_groups=same_core)  15 us
    all_to_all x1, starting transfers between devices, local(): lax.all_to_all(parts, ('row', 'col'), 0, 0, tiled=True, axis_index_groups...  8.45 us
    all_to_all x1, starting transfers between devices, local(): lax.all_to_all(jnp.broadcast_to(own, (PEERS,) + own.shape), 'row', 0, 0,...  8.32 us
    pallas_call x1, Pallas kernels, local(): pl.pallas_call(strips_kernel, in_specs=[VMEM] * 4, out_specs=[VMEM] * 4,...  7.05 us
    ppermute x1, starting transfers between devices, local(): above = lax.ppermute(low_edge, 'row', down)  3.66 us
    ppermute x1, waiting for transfers between devices, local(): from_right = lax.ppermute(to_left, 'col', left)  3.4 us
  transfers between devices with their start and end apart: 6, of which 2 were waited for; matrix products, arithmetic and copies ran while one was open for 3% of the time, Pallas kernels for 6%

commit v1 on v0

v1 whole, which is shorter than its diff:
```python
import functools

import jax
import jax.numpy as jnp
from jax import lax
from jax.experimental import pallas as pl
from jax.experimental.pallas import tpu as pltpu
from jax.sharding import PartitionSpec as P

C = 48
ROWS = 32
COLS = 128
HALO = 12
GHALO = 4
EXT = ROWS + 2 * HALO
GEXT = ROWS + 2 * GHALO
TAPS = 9 * C
BINS = 1024
PEERS = 16
F32 = jnp.float32
BF16 = jnp.bfloat16
VMEM = pl.BlockSpec(memory_space=pltpu.VMEM)
SMEM = pl.BlockSpec(memory_space=pltpu.SMEM)


def lanes_of(rows, width=COLS):
    return lax.broadcasted_iota(jnp.int32, (rows, width), 1)


def turn(value, shift):
    width = value.shape[-1]
    if isinstance(shift, int):
        shift = shift % width
        if shift == 0:
            return value
    return pltpu.roll(value, shift, value.ndim - 1)


def spread(first, second):
    low = lanes_of(C // 2) < 64
    top = jnp.where(low, first, turn(second, 64))
    bottom = jnp.where(low, turn(first, 64), second)
    return jnp.concatenate([top, bottom], axis=0)


def packed(value):
    low = lanes_of(C // 2) < 64
    top, bottom = value[: C // 2], value[C // 2 :]
    first = jnp.where(low, top, turn(bottom, 64))
    second = jnp.where(low, turn(top, 64), bottom)
    return first, second


def project_kernel(embed, proj_t, out):
    core = lax.axis_index("row") % 2
    part = lax.dot_general(
        proj_t[...], embed[...], (((1,), (1,)), ((), ())),
        precision=lax.Precision.HIGHEST, preferred_element_type=F32,
    )
    part = jnp.concatenate([part, jnp.zeros((C, COLS - ROWS), F32)], axis=1)
    mine = turn(part[: C // 2], 32 * core) + turn(part[C // 2 :], 64 + 32 * core)
    for peer in range(PEERS):
        out[peer] = mine


def source(e):
    if e < HALO:
        return 0, e
    if e < HALO + ROWS:
        return 1, e - HALO
    return 2, e - HALO - ROWS


def edges_kernel(pair, cot, low, high):
    for e in range(HALO):
        low[e] = pair[pl.ds(e + ROWS - HALO, C, stride=ROWS), :]
        high[e] = pair[pl.ds(e, C, stride=ROWS), :]
    for e in range(GHALO):
        low[e + HALO] = cot[pl.ds(e + ROWS - GHALO, C, stride=ROWS), :]
        high[e + HALO] = cot[pl.ds(e, C, stride=ROWS), :]


def combine_kernel(parts, out):
    total = parts[0]
    for peer in range(1, PEERS):
        total = total + parts[peer]
    for peer in range(PEERS):
        out[peer] = total


def strips_kernel(pair, cot, above, below, to_left, to_right):
    lane = lanes_of(C)
    for k in range(EXT // 8):
        left = jnp.zeros((C, COLS), F32)
        right = jnp.zeros((C, COLS), F32)
        for s in range(8):
            e = 8 * k + s
            where_, at = source(e)
            if where_ == 1:
                x = pair[pl.ds(at, C, stride=ROWS), :]
                g = cot[pl.ds(at, C, stride=ROWS), :]
            else:
                ref = (above, None, below)[where_]
                x = ref[at]
                g = None
                if 8 <= e < HALO:
                    g = above[HALO + e - 8]
                if HALO + ROWS <= e < HALO + ROWS + GHALO:
                    g = below[HALO + at]
            to_l, to_r = x, x
            if g is not None:
                to_l = jnp.where(lane < 12, x, turn(g, 12))
                to_r = jnp.where(lane < 116, turn(g, -12), x)
            slot = (lane >= 16 * s) & (lane < 16 * s + 16)
            left = jnp.where(slot, turn(to_l, 16 * s), left)
            right = jnp.where(slot, turn(to_r, 16 * s - 112), right)
        to_left[k] = left
        to_right[k] = right


def weights_kernel(taps, out):
    for m, (layer, flip) in enumerate(((0, False), (1, False), (1, True), (0, True))):
        tiles = [taps[9 * layer + n] for n in range(9)]
        if flip:
            tiles = [tile.T for tile in tiles]
        hi, lo = split(jnp.concatenate(tiles, axis=1))
        out[m, :C] = hi
        out[m, C:] = lo


def dot(a, b):
    return jnp.dot(a, b, preferred_element_type=F32)


def split(value):
    hi = value.astype(BF16)
    lo = (value - hi.astype(F32)).astype(BF16)
    return hi, lo


def weighted(weights, x_hi, x_lo):
    both = dot(weights, x_hi)
    low = dot(weights[:C], x_lo)
    return both[:C] + (both[C:] + low)


def main_kernel(
    dil, pair, cot, above, below, from_left, from_right, fields, wts, pair_out, send,
    x0, xh, xl, yh, yl, sh, sl, gm, gb, t0s, s0s, g1s, buf,
):
    d0, d1 = dil[0], dil[1]
    row, col = lax.axis_index("row"), lax.axis_index("col")
    lane = lanes_of(C)
    own_u = spread(fields[2 * col], fields[2 * col + 1])
    side_u = spread(fields[jnp.minimum(2 * col + 2, PEERS - 1)], fields[jnp.maximum(2 * col - 1, 0)])
    group, core = row // 2, row % 2
    near = jnp.clip(group - 1 + core, 0, PEERS - 1)
    far = jnp.clip(group + core, 0, PEERS - 1)
    row_u = turn(spread(fields[near], fields[far]), 76 + 32 * core)
    inside = ((lane < HALO) & (col < 7)) | ((lane >= COLS - HALO) & (col > 0))
    side_mask = jnp.where(inside, 1.0, 0.0).astype(F32)
    side_u = side_u * side_mask

    def row_mask(e):
        at = row * ROWS + e - HALO
        return jnp.where((at >= 0) & (at < BINS), 1.0, 0.0).astype(F32)

    def put_shifted(hi_ref, lo_ref, e, main, side, step, swap):
        low = lane < step
        high = lane >= COLS - step
        for ref, a, b in zip((hi_ref, lo_ref), split(main), split(side)):
            a_up, b_up = turn(a, step), turn(b, step)
            a_down, b_down = turn(a, COLS - step), turn(b, COLS - step)
            up = jnp.where(low, b_up, a_up)
            down = jnp.where(high, b_down, a_down)
            if swap:
                ref[e, :C] = down
                ref[e, C : 2 * C] = a
                ref[e, 2 * C :] = up
            else:
                ref[e, :C, :COLS] = up
                ref[e, :C, COLS:] = jnp.where(low, a_up, b_up)
                ref[e, C : 2 * C, :COLS] = a
                ref[e, C : 2 * C, COLS:] = b
                ref[e, 2 * C :, :COLS] = down
                ref[e, 2 * C :, COLS:] = jnp.where(high, a_down, b_down)

    def assemble(e, k, s, x, ur):
        fl, fr = from_left[k], from_right[k]
        keep = row_mask(e)
        ui = jnp.broadcast_to(ur, (C, COLS)) * keep
        main = x + (ui + own_u * keep)
        side = jnp.where(
            lane < HALO, turn(fr, -16 * s),
            jnp.where(lane >= COLS - HALO, turn(fl, 112 - 16 * s), 0.0),
        )
        side = side + (ui * side_mask + side_u * keep)
        x0[e, :, :COLS] = main
        x0[e, :, COLS:] = side
        put_shifted(xh, xl, e, main, side, d0, False)

    def assemble_g(f, k, s, g):
        gm[f] = g
        gb[f] = jnp.where(
            lane < GHALO, turn(from_right[k], -(16 * s + 12)),
            jnp.where(lane >= COLS - GHALO, turn(from_left[k], 124 - 16 * s), 0.0),
        )

    for e in tuple(range(HALO)) + tuple(range(HALO + ROWS, EXT)):
        where_, at = source(e)
        ref = above if where_ == 0 else below
        assemble(e, e // 8, e % 8, ref[at], row_u[:, e : e + 1])
        if 8 <= e < HALO:
            assemble_g(e - 8, e // 8, e % 8, above[HALO + e - 8])
        if HALO + ROWS <= e < HALO + ROWS + GHALO:
            assemble_g(e - 8, e // 8, e % 8, below[HALO + at])

    def assemble_own(q, carry):
        ur = turn(row_u, (COLS - HALO - 8 * q) % COLS)
        for s in range(8):
            k, slot = q + 1 + (s + 4) // 8, (s + 4) % 8
            at = 8 * q + s
            assemble(at + HALO, k, slot, pair[pl.ds(at, C, stride=ROWS), :], ur[:, s : s + 1])
            assemble_g(at + GHALO, k, slot, cot[pl.ds(at, C, stride=ROWS), :])
        return carry

    lax.fori_loop(0, ROWS // 8, assemble_own, 0)

    def stacked(ref, lowest, middle, highest):
        return jnp.concatenate([ref[lowest], ref[middle], ref[highest]], axis=0)

    def first(i, carry):
        e = i + 4
        acc = weighted(
            wts[0], stacked(xh, e - d0, e, e + d0), stacked(xl, e - d0, e, e + d0)
        )
        t = jnp.tanh(acc)
        t0s[e] = t[:, :COLS]
        keep = row_mask(e)
        main = x0[e, :, :COLS] + t[:, :COLS] * keep
        side = x0[e, :, COLS:] + t[:, COLS:] * (side_mask * keep)
        x0[e, :, :COLS] = main
        put_shifted(yh, yl, e, main, side, d1, False)
        return carry

    lax.fori_loop(0, EXT - 8, first, 0, unroll=16)

    def second(e, own):
        acc = weighted(
            wts[1], stacked(yh, e - d1, e, e + d1), stacked(yl, e - d1, e, e + d1)
        )
        t = jnp.tanh(acc)
        if own:
            pair_out[pl.ds(e - HALO, C, stride=ROWS), :] = x0[e, :, :COLS] + t[:, :COLS]
        slope = 1.0 - t * t
        put_shifted(sh, sl, e - 8, gm[e - 8] * slope[:, :COLS], gb[e - 8] * slope[:, COLS:], d1, True)

    def second_own(i, carry):
        second(i + HALO, True)
        return carry

    for e in (8, 9, 10, 11, 44, 45, 46, 47):
        second(e, False)
    lax.fori_loop(0, ROWS, second_own, 0, unroll=16)

    def third(i, carry):
        parts_hi, parts_lo = [], []
        for k in range(2):
            q = 2 * i + k + GHALO
            parts_hi.append(stacked(sh, q + d1, q, q - d1))
            parts_lo.append(stacked(sl, q + d1, q, q - d1))
        acc = weighted(
            wts[2], jnp.concatenate(parts_hi, axis=1), jnp.concatenate(parts_lo, axis=1)
        )
        for k in range(2):
            at = 2 * i + k
            g1 = gm[at + GHALO] + acc[:, k * COLS : (k + 1) * COLS]
            t = t0s[at + HALO]
            g1s[at] = g1
            s0s[at] = g1 * (1.0 - t * t)
        return carry

    lax.fori_loop(0, ROWS // 2, third, 0, unroll=8)

    lane8 = lanes_of(8)
    edge = ((lane8 < d0) & (col == 0)) | ((lane8 >= COLS - d0) & (col == 7))
    edge_lanes = jnp.where(edge, 1.0, 0.0).astype(F32)
    first_col = jnp.where(col == 0, 1.0, 0.0).astype(F32)
    last_col = jnp.where(col == 7, 1.0, 0.0).astype(F32)
    pieces = []
    for octet in range(C // 8):
        at = slice(8 * octet, 8 * octet + 8)
        cg = c0 = rg = r0 = re = top = bottom = jnp.zeros((8, COLS), F32)
        for i in range(ROWS):
            s0, g1 = s0s[i, at], g1s[i, at]
            cg, c0 = cg + g1, c0 + s0
            here = lane8 == i
            rg = jnp.where(here, jnp.sum(g1, axis=1, keepdims=True), rg)
            r0 = jnp.where(here, jnp.sum(s0, axis=1, keepdims=True), r0)
            re = jnp.where(here, jnp.sum(s0 * edge_lanes, axis=1, keepdims=True), re)
            if i < GHALO:
                top = top + s0 * jnp.where((row == 0) & (i < d0), 1.0, 0.0).astype(F32)
            if i >= ROWS - GHALO:
                bottom = bottom + s0 * jnp.where((row == 31) & (i >= ROWS - d0), 1.0, 0.0).astype(F32)
        pieces.append((cg, c0 - top, c0, c0 - bottom, rg, r0 - re * first_col, r0, r0 - re * last_col))
    cg, cd, c0, cu, rg, rd, r0, ru = [jnp.concatenate(p, axis=0) for p in zip(*pieces)]
    zero = jnp.zeros((C, COLS), F32)
    blocks = []
    for part in (cd, c0, cu):
        wide = jnp.concatenate([part, zero], axis=1)
        blocks += [turn(wide, 256 - d0), wide, turn(wide, d0)]
    col_x = jnp.concatenate(blocks, axis=0)
    blocks = []
    for a in range(3):
        for part in (rd, r0, ru):
            blocks.append((turn(part, COLS - d0), part, turn(part, d0))[a])
    row_x = jnp.concatenate(blocks, axis=0)
    hi, lo = split(jnp.concatenate([col_x, row_x], axis=1))
    made = weighted(wts[3], hi, lo)
    buf[...] = jnp.zeros(buf.shape, F32)

    def add(first_at, second_at, value):
        one, two = packed(value)
        buf[first_at] = buf[first_at] + one
        buf[second_at] = buf[second_at] + two

    add(2 * col + 1, 2 * col + 2, cg + made[:, :COLS])
    add(2 * col + 3, 2 * col, made[:, COLS : 2 * COLS])
    add(group + core, group + core + 1, turn(rg + made[:, 2 * COLS :], 64 - 32 * core))
    send[...] = buf[1 : PEERS + 1]


def layers(dilation, pair, cot, above, below, from_left, from_right, fields, wts):
    return pl.pallas_call(
        main_kernel,
        in_specs=[SMEM] + [VMEM] * 8,
        out_specs=[VMEM] * 2,
        out_shape=[
            jax.ShapeDtypeStruct((C * ROWS, COLS), F32),
            jax.ShapeDtypeStruct((PEERS, C // 2, COLS), F32),
        ],
        scratch_shapes=[
            pltpu.VMEM((EXT, C, 2 * COLS), F32),
            pltpu.VMEM((EXT, 3 * C, 2 * COLS), BF16),
            pltpu.VMEM((EXT, 3 * C, 2 * COLS), BF16),
            pltpu.VMEM((EXT, 3 * C, 2 * COLS), BF16),
            pltpu.VMEM((EXT, 3 * C, 2 * COLS), BF16),
            pltpu.VMEM((GEXT, 3 * C, COLS), BF16),
            pltpu.VMEM((GEXT, 3 * C, COLS), BF16),
            pltpu.VMEM((GEXT, C, COLS), F32),
            pltpu.VMEM((GEXT, C, COLS), F32),
            pltpu.VMEM((EXT, C, COLS), F32),
            pltpu.VMEM((ROWS, C, COLS), F32),
            pltpu.VMEM((ROWS, C, COLS), F32),
            pltpu.VMEM((PEERS + 2, C // 2, COLS), F32),
        ],
        compiler_params=pltpu.CompilerParams(vmem_limit_bytes=40 * 2**20),
        name="layers",
    )(dilation, pair, cot, above, below, from_left, from_right, fields, wts)


def finish_kernel(parts, proj_t, out):
    core = lax.axis_index("row") % 2
    total = parts[0]
    for peer in range(1, PEERS):
        total = total + parts[peer]
    both = jnp.concatenate([turn(total, 128 - 32 * core), turn(total, 64 - 32 * core)], axis=0)
    grad = lax.dot_general(
        both, proj_t[...], (((0,), (0,)), ((), ())),
        precision=lax.Precision.HIGHEST, preferred_element_type=F32,
    )
    out[...] = grad[:ROWS]


def local(embed, proj, pair_in, kernels, dilation, cotangent):
    rows, cols = 32, 8
    down = [(i, i + 1) for i in range(rows - 1)]
    up = [(i + 1, i) for i in range(rows - 1)]
    right = [(i, i + 1) for i in range(cols - 1)]
    left = [(i + 1, i) for i in range(cols - 1)]
    same_core = [[2 * i + core for i in range(PEERS)] for core in range(2)]
    chips = [[(2 * g + core) * cols + c for core in range(2) for c in range(cols)] for g in range(PEERS)]
    packs = jax.ShapeDtypeStruct((PEERS, C // 2, COLS), F32)
    proj_t = proj.T

    pair = pair_in.reshape(C * ROWS, COLS)
    cot = cotangent.reshape(C * ROWS, COLS)
    low_edge, high_edge = pl.pallas_call(
        edges_kernel, in_specs=[VMEM] * 2, out_specs=[VMEM] * 2,
        out_shape=[jax.ShapeDtypeStruct((HALO + GHALO, C, COLS), F32)] * 2, name="edges",
        compiler_params=pltpu.CompilerParams(vmem_limit_bytes=8 * 2**20),
    )(pair, cot)
    low_edge, high_edge, embed = lax.optimization_barrier((low_edge, high_edge, embed))
    above = lax.ppermute(low_edge, "row", down)
    below = lax.ppermute(high_edge, "row", up)

    parts = pl.pallas_call(
        project_kernel, in_specs=[VMEM, VMEM], out_specs=VMEM, out_shape=packs, name="project",
    )(embed, proj_t)
    parts = lax.all_to_all(parts, ("row", "col"), 0, 0, tiled=True, axis_index_groups=chips)

    to_left, to_right = pl.pallas_call(
        strips_kernel,
        in_specs=[VMEM] * 4,
        out_specs=[VMEM] * 2,
        out_shape=[jax.ShapeDtypeStruct((EXT // 8, C, COLS), F32)] * 2,
        compiler_params=pltpu.CompilerParams(vmem_limit_bytes=8 * 2**20),
        name="strips",
    )(pair, cot, above, below)
    parts, to_left, to_right = lax.optimization_barrier((parts, to_left, to_right))
    from_left = lax.ppermute(to_right, "col", right)
    from_right = lax.ppermute(to_left, "col", left)

    fields = pl.pallas_call(
        combine_kernel, in_specs=[VMEM], out_specs=VMEM, out_shape=packs, name="combine",
        cost_estimate=pl.CostEstimate(flops=0, transcendentals=0, bytes_accessed=64 * 2**20),
    )(parts)
    fields = lax.all_to_all(fields, "row", 0, 0, tiled=True, axis_index_groups=same_core)

    taps = kernels.transpose(0, 3, 4, 1, 2).reshape(18, C, C)
    wts = pl.pallas_call(
        weights_kernel, in_specs=[VMEM], out_specs=VMEM,
        out_shape=jax.ShapeDtypeStruct((4, 2 * C, TAPS), BF16), name="weights",
    )(taps)
    pair_out, send = layers(dilation, pair, cot, above, below, from_left, from_right, fields, wts)

    got = lax.all_to_all(send, "row", 0, 0, tiled=True, axis_index_groups=same_core)
    own = jnp.sum(got, axis=0)
    got = lax.all_to_all(
        jnp.broadcast_to(own, (PEERS,) + own.shape), ("row", "col"), 0, 0, tiled=True, axis_index_groups=chips
    )
    embed_grad = pl.pallas_call(
        finish_kernel, in_specs=[VMEM, VMEM], out_specs=VMEM,
        out_shape=jax.ShapeDtypeStruct((ROWS, 64), F32), name="finish",
    )(got, proj_t)
    return (pair_out.reshape(C, ROWS, COLS), embed_grad)


def solution(mesh):
    in_specs = (
        P("row", "col"),
        P("col", None),
        P(None, "row", "col"),
        P(),
        P(),
        P(None, "row", "col"),
    )
    out_specs = (P(None, "row", "col"), P("row", "col"))
    return jax.shard_map(local, mesh=mesh, in_specs=in_specs, out_specs=out_specs, check_vma=False)
```

time: 114 us -> 105 us (0.921)
  Pallas kernels: 36.7 us -> 29.6 us
  waiting for transfers between devices: 5.09 us -> 8.63 us
  blocking collectives: 37.1 us -> 34.3 us
  other arithmetic: 2.23 us -> 0.02 us
  local copies, waits for them, and re-layouts: 5.72 us -> 3.96 us
  starting transfers between devices: 25.8 us -> 27 us
    pallas_call x4 -> x7, Pallas kernels: 36.7 us -> 29.6 us  [the longest x1 18.4 us: layers(): pl.pallas_call(main_kernel, in_specs=[SMEM] + [VMEM] * 8, out_specs=[VMEM...]
    all_to_all x1, waiting for transfers between devices: 1.68 us -> 5.06 us  [local(): lax.all_to_all(parts, ('row', 'col'), 0, 0, tiled=True, axis_index_groups...]
    all_to_all x1, blocking collectives: 22.1 us -> 19.8 us  [local(): lax.all_to_all(jnp.broadcast_to(own, (PEERS,) + own.shape), ('row', 'col'...]
    another operation x2 -> x0, other arithmetic: 2.07 us -> none  [the longest x1 1.29 us: local(): scal = jnp.stack([dilation[0], dilation[1], row, col]).astype(jnp.int32)]
    slice x10 -> x0, local copies, waits for them, and re-layouts: 1.99 us -> none  [the longest x1 1.06 us: local(): cotangent[:, :GHALO]]
    all_to_all x1, starting transfers between devices: 8.45 us -> 7.06 us  [local(): lax.all_to_all(parts, ('row', 'col'), 0, 0, tiled=True, axis_index_groups...]
    all_to_all x1, starting transfers between devices: 8.32 us -> 9.62 us  [local(): lax.all_to_all(fields, 'row', 0, 0, tiled=True, axis_index_groups=same_core)]
    ppermute x1, starting transfers between devices: 3.66 us -> 4.94 us  [local(): above = lax.ppermute(low_edge, 'row', down)]
  transfers between devices with their start and end apart: 6 -> 6, of which waited for: 2 -> 2; matrix products, arithmetic and copies ran while one was open for 3% -> 0% of each run, Pallas kernels for 6% -> 7%
where the time goes in v1:
time: 105 us; the launch traced here: 104 us
  blocking collectives  34.3 us (33%)
  Pallas kernels  29.6 us (28%)
  starting transfers between devices  27 us (26%)
  waiting for transfers between devices  8.63 us (8%)
  local copies, waits for them, and re-layouts  3.96 us (4%)
    all_to_all x1, blocking collectives, local(): lax.all_to_all(jnp.broadcast_to(own, (PEERS,) + own.shape), ('row', 'col'...  19.8 us
    pallas_call x1, Pallas kernels, layers(): pl.pallas_call(main_kernel, in_specs=[SMEM] + [VMEM] * 8, out_specs=[VMEM...  18.4 us
    all_to_all x1, blocking collectives, local(): lax.all_to_all(send, 'row', 0, 0, tiled=True, axis_index_groups=same_core)  14.5 us
    all_to_all x1, starting transfers between devices, local(): lax.all_to_all(fields, 'row', 0, 0, tiled=True, axis_index_groups=same_core)  9.62 us
    all_to_all x1, starting transfers between devices, local(): lax.all_to_all(parts, ('row', 'col'), 0, 0, tiled=True, axis_index_groups...  7.06 us
    all_to_all x1, waiting for transfers between devices, local(): lax.all_to_all(parts, ('row', 'col'), 0, 0, tiled=True, axis_index_groups...  5.06 us
    ppermute x1, starting transfers between devices, local(): above = lax.ppermute(low_edge, 'row', down)  4.94 us
    unnamed x14, local copies, waits for them, and re-layouts  3.94 us
  transfers between devices with their start and end apart: 6, of which 2 were waited for; matrix products, arithmetic and copies ran while one was open for 0% of the time, Pallas kernels for 7%

profile of v1, /device:TPU:1, one launch (start us, length us, event | category | flops | bytes accessed | tf_op | source)
XLA Modules:
  0.0 104.3 jit_solution(6247921754690443839)
XLA Ops:
  0.6 0.0 copy-start
  0.6 1.1 %copy-done = f32[48,32,128]{2,1,0:T(8,128)S(1)} copy-done((f32[48,32,128]{2,1,0:T(8,128)S(1)}, f32[48,32,128]{2,1,0:T(8,128)}, u32[]{:S(2)}) %copy-start) | copy-done | bytes 786456
  1.8 0.0 copy-start.2
  1.8 1.1 %copy-done.2 = f32[48,32,128]{2,1,0:T(8,128)S(1)} copy-done((f32[48,32,128]{2,1,0:T(8,128)S(1)}, f32[48,32,128]{2,1,0:T(8,128)}, u32[]{:S(2)}) %copy-start.2) | copy-done | bytes 786456
  2.9 0.0 copy-start.1
  2.9 0.0 copy-start.3
  2.9 0.5 edges.1
  3.4 4.9 %collective-permute-start = (f32[16,48,128]{2,1,0:T(8,128)S(1)}, f32[16,48,128]{2,1,0:T(8,128)S(1)}, u32[]{:S(2)}, u32[]{:S(2)}) collective-permute-start(f32[16,48,128]{2,1,0:T(8,128)S(1)} %get-tuple-element.16), channel_id=1, source_target_pairs={{0,8},{8,16},{16,24},{24,32},{32,40},{40,48},{48,56},{56,64},{64,7... | collective-permute-start | bytes 1179656 | tf_op jit(solution)/shard_map/ppermute | solution.py:394
  8.3 1.9 %collective-permute-start.1 = (f32[16,48,128]{2,1,0:T(8,128)S(1)}, f32[16,48,128]{2,1,0:T(8,128)S(1)}, u32[]{:S(2)}, u32[]{:S(2)}) collective-permute-start(f32[16,48,128]{2,1,0:T(8,128)S(1)} %get-tuple-element.17), channel_id=1, source_target_pairs={{8,0},{16,8},{24,16},{32,24},{40,32},{48,40},{56,48},{64,56},{72,6... | collective-permute-start | bytes 1179656 | tf_op jit(solution)/shard_map/ppermute | solution.py:395
  10.2 1.7 %project.1 = f32[16,24,128]{2,1,0:T(8,128)} custom-call(f32[32,64]{1,0:T(8,128)} %embed, f32[48,64]{1,0:T(8,128)} %bitcast.14), custom_call_target="tpu_custom_call" | custom-call | tf_op jit(solution)/shard_map/project/pallas_call | solution.py:397
  11.9 7.1 %all-to-all-start = ((f32[16,24,128]{2,1,0:T(8,128)}), f32[16,24,128]{2,1,0:T(8,128)S(1)}, u32[]{:S(2)}, u32[]{:S(2)}) async-start(f32[16,24,128]{2,1,0:T(8,128)} %project.1), calls=%async_computation | async-start | bytes 393216 | tf_op jit(solution)/shard_map/all_to_all | solution.py:400
  19.0 0.0 collective-permute-done.above
  19.0 0.0 collective-permute-done.1.below
  19.0 0.0 copy-done.1
  19.0 0.0 copy-done.3
  19.0 3.4 %strips.1 = (f32[7,48,128]{2,1,0:T(8,128)S(1)}, f32[7,48,128]{2,1,0:T(8,128)S(1)}) custom-call(f32[1536,128]{1,0:T(8,128)S(1)} %bitcast.8, f32[1536,128]{1,0:T(8,128)S(1)} %bitcast.11, f32[16,48,128]{2,1,0:T(8,128)S(1)} %collective-permute-done.above, f32[16,48,128]{2,1,0:T(8,128)S(1)} %collective-permute-done.1.below), custom_call_target="tpu_custom_call" | custom-call | tf_op jit(solution)/shard_map/strips/pallas_call | solution.py:402
  22.4 5.1 %all-to-all-done.parts = f32[16,24,128]{2,1,0:T(8,128)S(1)} async-done(((f32[16,24,128]{2,1,0:T(8,128)}), f32[16,24,128]{2,1,0:T(8,128)S(1)}, u32[]{:S(2)}, u32[]{:S(2)}) %all-to-all-start) | async-done | bytes 196640 | tf_op jit(solution)/shard_map/all_to_all | solution.py:400
  27.5 0.0 copy-start.6
  27.5 0.7 copy-done.6
  28.2 1.6 %combine.1 = f32[16,24,128]{2,1,0:T(8,128)} custom-call(f32[16,24,128]{2,1,0:T(8,128)} %copy-done.6), custom_call_target="tpu_custom_call" | custom-call | bytes 67108864 | tf_op jit(solution)/shard_map/combine/pallas_call | solution.py:414
  29.8 9.6 %all-to-all-start.1 = ((f32[16,24,128]{2,1,0:T(8,128)}), f32[16,24,128]{2,1,0:T(8,128)S(1)}, u32[]{:S(2)}, u32[]{:S(2)}) async-start(f32[16,24,128]{2,1,0:T(8,128)} %combine.1), calls=%async_computation.1 | async-start | bytes 393216 | tf_op jit(solution)/shard_map/all_to_all | solution.py:418
  39.5 2.2 %collective-permute-start.2 = (f32[7,48,128]{2,1,0:T(8,128)S(1)}, f32[7,48,128]{2,1,0:T(8,128)S(1)}, u32[]{:S(2)}, u32[]{:S(2)}) collective-permute-start(f32[7,48,128]{2,1,0:T(8,128)S(1)} %get-tuple-element.21), channel_id=1, source_target_pairs={{0,1},{1,2},{2,3},{3,4},{4,5},{5,6},{6,7},{8,9},{9,10},{10,11},{11... | collective-permute-start | bytes 516104 | tf_op jit(solution)/shard_map/ppermute | solution.py:411
  41.7 1.3 %collective-permute-start.3 = (f32[7,48,128]{2,1,0:T(8,128)S(1)}, f32[7,48,128]{2,1,0:T(8,128)S(1)}, u32[]{:S(2)}, u32[]{:S(2)}) collective-permute-start(f32[7,48,128]{2,1,0:T(8,128)S(1)} %get-tuple-element.22), channel_id=1, source_target_pairs={{1,0},{2,1},{3,2},{4,3},{5,4},{6,5},{7,6},{9,8},{10,9},{11,10},{12... | collective-permute-start | bytes 516104 | tf_op jit(solution)/shard_map/ppermute | solution.py:412
  43.0 0.0 copy-start.5
  43.0 2.1 %weights.1.wts = bf16[4,96,432]{2,1,0:T(8,128)(2,1)} custom-call(f32[18,48,48]{2,1,0:T(8,128)} %bitcast.13), custom_call_target="tpu_custom_call" | custom-call | tf_op jit(solution)/shard_map/weights/pallas_call | solution.py:421
  45.1 0.0 collective-permute-done.2.from_left
  45.1 3.6 %collective-permute-done.3.from_right = f32[7,48,128]{2,1,0:T(8,128)S(1)} collective-permute-done((f32[7,48,128]{2,1,0:T(8,128)S(1)}, f32[7,48,128]{2,1,0:T(8,128)S(1)}, u32[]{:S(2)}, u32[]{:S(2)}) %collective-permute-start.3) | collective-permute-done | bytes 172064 | tf_op jit(solution)/shard_map/ppermute | solution.py:412
  48.7 0.0 all-to-all-done.1.fields
  48.7 0.0 copy-done.5
  48.7 0.0 copy-start.4
  48.7 1.0 copy-done.4
  49.7 18.4 %layers.1 = (f32[1536,128]{1,0:T(8,128)}, f32[16,24,128]{2,1,0:T(8,128)S(1)}) custom-call(s32[2]{0:T(128)S(1)} %copy-done.5, f32[1536,128]{1,0:T(8,128)S(1)} %bitcast.9, f32[1536,128]{1,0:T(8,128)S(1)} %bitcast.12, f32[16,48,128]{2,1,0:T(8,128)S(1)} %collective-permute-done.above, f32[16,48,128]{2,1,0:T(8,128)S(1)} %collective-permute-done.1.below, ...), custom_call_target="tpu_custom_call" | custom-call | tf_op jit(solution)/shard_map/layers/pallas_call | solution.py:334
  68.1 14.5 %all_to_all.20 = f32[16,24,128]{2,1,0:T(8,128)S(1)} all-to-all(f32[16,24,128]{2,1,0:T(8,128)S(1)} %get-tuple-element.25), channel_id=1, replica_groups={{0,16,32,48,64,80,96,112,128,144,160,176,192,208,224,240},{8,24,40,56,7..., dimensions={0} | all-to-all | bytes 393216 | tf_op jit(solution)/shard_map/all_to_all | solution.py:427
  82.7 19.8 %all_to_all.21.parts = f32[16,24,128]{2,1,0:T(8,128)} all-to-all(f32[16,24,128]{2,1,0:T(8,128)S(1)} %broadcast_in_dim.3), channel_id=1, replica_groups={{0,1,2,3,4,5,6,7,8,9,10,11,12,13,14,15},{16,17,18,19,20,21,22,23,24,25,..., dimensions={0} | all-to-all | bytes 393216 | tf_op jit(solution)/shard_map/all_to_all | solution.py:429
  102.5 1.9 %finish.1 = f32[32,64]{1,0:T(8,128)} custom-call(f32[16,24,128]{2,1,0:T(8,128)} %all_to_all.21.parts, f32[48,64]{1,0:T(8,128)} %bitcast.15), custom_call_target="tpu_custom_call" | custom-call | tf_op jit(solution)/shard_map/finish/pallas_call | solution.py:432
  (2 shorter events, 0.0 us)
Async XLA Ops:
  0.6 1.1 %copy-start = (f32[48,32,128]{2,1,0:T(8,128)S(1)}, f32[48,32,128]{2,1,0:T(8,128)}, u32[]{:S(2)}) copy-start(f32[48,32,128]{2,1,0:T(8,128)} %param.8) | copy-start | bytes 2359300
  1.8 1.1 %copy-start.2 = (f32[48,32,128]{2,1,0:T(8,128)S(1)}, f32[48,32,128]{2,1,0:T(8,128)}, u32[]{:S(2)}) copy-start(f32[48,32,128]{2,1,0:T(8,128)} %param.11) | copy-start | bytes 2359300
  2.9 16.1 %copy-start.1 = (f32[48,32,128]{2,1,0:T(8,128)S(1)}, f32[48,32,128]{2,1,0:T(8,128)}, u32[]{:S(2)}) copy-start(f32[48,32,128]{2,1,0:T(8,128)} %param.8) | copy-start | bytes 2359300
  2.9 16.1 %copy-start.3 = (f32[48,32,128]{2,1,0:T(8,128)S(1)}, f32[48,32,128]{2,1,0:T(8,128)}, u32[]{:S(2)}) copy-start(f32[48,32,128]{2,1,0:T(8,128)} %param.11) | copy-start | bytes 2359300
  3.4 15.6 %collective-permute-start = (f32[16,48,128]{2,1,0:T(8,128)S(1)}, f32[16,48,128]{2,1,0:T(8,128)S(1)}, u32[]{:S(2)}, u32[]{:S(2)}) collective-permute-start(f32[16,48,128]{2,1,0:T(8,128)S(1)} %get-tuple-element.16), channel_id=1, source_target_pairs={{0,8},{8,16},{16,24},{24,32},{32,40},{40,48},{48,56},{56,64},{64,7... | collective-permute-start | bytes 1179656 | tf_op jit(solution)/shard_map/ppermute | solution.py:394
  8.3 10.7 %collective-permute-start.1 = (f32[16,48,128]{2,1,0:T(8,128)S(1)}, f32[16,48,128]{2,1,0:T(8,128)S(1)}, u32[]{:S(2)}, u32[]{:S(2)}) collective-permute-start(f32[16,48,128]{2,1,0:T(8,128)S(1)} %get-tuple-element.17), channel_id=1, source_target_pairs={{8,0},{16,8},{24,16},{32,24},{40,32},{48,40},{56,48},{64,56},{72,6... | collective-permute-start | bytes 1179656 | tf_op jit(solution)/shard_map/ppermute | solution.py:395
  11.9 15.6 %all-to-all-start = ((f32[16,24,128]{2,1,0:T(8,128)}), f32[16,24,128]{2,1,0:T(8,128)S(1)}, u32[]{:S(2)}, u32[]{:S(2)}) async-start(f32[16,24,128]{2,1,0:T(8,128)} %project.1), calls=%async_computation | async-start | bytes 393216 | tf_op jit(solution)/shard_map/all_to_all | solution.py:400
  27.5 0.7 copy-start.6
  29.8 18.9 %all-to-all-start.1 = ((f32[16,24,128]{2,1,0:T(8,128)}), f32[16,24,128]{2,1,0:T(8,128)S(1)}, u32[]{:S(2)}, u32[]{:S(2)}) async-start(f32[16,24,128]{2,1,0:T(8,128)} %combine.1), calls=%async_computation.1 | async-start | bytes 393216 | tf_op jit(solution)/shard_map/all_to_all | solution.py:418
  39.5 5.7 %collective-permute-start.2 = (f32[7,48,128]{2,1,0:T(8,128)S(1)}, f32[7,48,128]{2,1,0:T(8,128)S(1)}, u32[]{:S(2)}, u32[]{:S(2)}) collective-permute-start(f32[7,48,128]{2,1,0:T(8,128)S(1)} %get-tuple-element.21), channel_id=1, source_target_pairs={{0,1},{1,2},{2,3},{3,4},{4,5},{5,6},{6,7},{8,9},{9,10},{10,11},{11... | collective-permute-start | bytes 516104 | tf_op jit(solution)/shard_map/ppermute | solution.py:411
  41.7 7.0 %collective-permute-start.3 = (f32[7,48,128]{2,1,0:T(8,128)S(1)}, f32[7,48,128]{2,1,0:T(8,128)S(1)}, u32[]{:S(2)}, u32[]{:S(2)}) collective-permute-start(f32[7,48,128]{2,1,0:T(8,128)S(1)} %get-tuple-element.22), channel_id=1, source_target_pairs={{1,0},{2,1},{3,2},{4,3},{5,4},{6,5},{7,6},{9,8},{10,9},{11,10},{12... | collective-permute-start | bytes 516104 | tf_op jit(solution)/shard_map/ppermute | solution.py:412
  43.0 5.7 %copy-start.5 = (s32[2]{0:T(128)S(1)}, s32[2]{0:T(128)}, u32[]{:S(2)}) copy-start(s32[2]{0:T(128)} %dil.1) | copy-start | bytes 28
  48.7 1.0 copy-start.4

commit v2 on v1

--- a/solution.py
+++ b/solution.py
@@ -63,6 +63,11 @@
         out[peer] = mine
 
 
+def partners(mine_is_even, got_a, got_b, at):
+    one, two = got_a[at], got_b[at]
+    return jnp.where(mine_is_even, two, one), jnp.where(mine_is_even, one, two)
+
+
 def source(e):
     if e < HALO:
         return 0, e
@@ -71,42 +76,38 @@
     return 2, e - HALO - ROWS
 
 
-def edges_kernel(pair, cot, low, high):
-    for e in range(HALO):
-        low[e] = pair[pl.ds(e + ROWS - HALO, C, stride=ROWS), :]
-        high[e] = pair[pl.ds(e, C, stride=ROWS), :]
-    for e in range(GHALO):
-        low[e + HALO] = cot[pl.ds(e + ROWS - GHALO, C, stride=ROWS), :]
-        high[e + HALO] = cot[pl.ds(e, C, stride=ROWS), :]
-
-
-def combine_kernel(parts, out):
-    total = parts[0]
-    for peer in range(1, PEERS):
-        total = total + parts[peer]
-    for peer in range(PEERS):
-        out[peer] = total
-
-
-def strips_kernel(pair, cot, above, below, to_left, to_right):
+def edges_kernel(pair, cot, to_a, to_b):
+    even = lax.axis_index("row") % 2 == 0
+    for ref, count, start in ((pair, HALO, 0), (cot, GHALO, HALO)):
+        for e in range(count):
+            low = ref[pl.ds(e + ROWS - count, C, stride=ROWS), :]
+            high = ref[pl.ds(e, C, stride=ROWS), :]
+            to_a[start + e] = jnp.where(even, low, high)
+            to_b[start + e] = jnp.where(even, high, low)
+
+
+def strips_kernel(pair, cot, got_a, got_b, to_a, to_b):
     lane = lanes_of(C)
+    row_even = lax.axis_index("row") % 2 == 0
+    col_even = lax.axis_index("col") % 2 == 0
     for k in range(EXT // 8):
         left = jnp.zeros((C, COLS), F32)
         right = jnp.zeros((C, COLS), F32)
         for s in range(8):
             e = 8 * k + s
-            where_, at = source(e)
-            if where_ == 1:
+            place, at = source(e)
+            g = None
+            if place == 1:
                 x = pair[pl.ds(at, C, stride=ROWS), :]
                 g = cot[pl.ds(at, C, stride=ROWS), :]
+            elif place == 0:
+                x = partners(row_even, got_a, got_b, at)[0]
+                if e >= 8:
+                    g = partners(row_even, got_a, got_b, HALO + e - 8)[0]
             else:
-                ref = (above, None, below)[where_]
-                x = ref[at]
-                g = None
-                if 8 <= e < HALO:
-                    g = above[HALO + e - 8]
-                if HALO + ROWS <= e < HALO + ROWS + GHALO:
-                    g = below[HALO + at]
+                x = partners(row_even, got_a, got_b, at)[1]
+                if at < GHALO:
+                    g = partners(row_even, got_a, got_b, HALO + at)[1]
             to_l, to_r = x, x
             if g is not None:
                 to_l = jnp.where(lane < 12, x, turn(g, 12))
@@ -114,8 +115,8 @@
             slot = (lane >= 16 * s) & (lane < 16 * s + 16)
             left = jnp.where(slot, turn(to_l, 16 * s), left)
             right = jnp.where(slot, turn(to_r, 16 * s - 112), right)
-        to_left[k] = left
-        to_right[k] = right
+        to_a[k] = jnp.where(col_even, right, left)
+        to_b[k] = jnp.where(col_even, left, right)
 
 
 def weights_kernel(taps, out):
@@ -145,12 +146,13 @@
 
 
 def main_kernel(
-    dil, pair, cot, above, below, from_left, from_right, fields, wts, pair_out, send,
-    x0, xh, xl, yh, yl, sh, sl, gm, gb, t0s, s0s, g1s, buf,
+    dil, pair, cot, row_a, row_b, col_a, col_b, fields, wts, pair_out, send,
+    x0, xh, xl, yh, yl, sh, sl, gm, sides, merged, t0s, s0s, g1s, buf,
 ):
     d0, d1 = dil[0], dil[1]
     row, col = lax.axis_index("row"), lax.axis_index("col")
     lane = lanes_of(C)
+    row_even, col_even = row % 2 == 0, col % 2 == 0
     own_u = spread(fields[2 * col], fields[2 * col + 1])
     side_u = spread(fields[jnp.minimum(2 * col + 2, PEERS - 1)], fields[jnp.maximum(2 * col - 1, 0)])
     group, core = row // 2, row % 2
@@ -169,59 +171,65 @@
         low = lane < step
         high = lane >= COLS - step
         for ref, a, b in zip((hi_ref, lo_ref), split(main), split(side)):
-            a_up, b_up = turn(a, step), turn(b, step)
-            a_down, b_down = turn(a, COLS - step), turn(b, COLS - step)
-            up = jnp.where(low, b_up, a_up)
-            down = jnp.where(high, b_down, a_down)
+            up = turn(jnp.where(high, b, a), step)
+            down = turn(jnp.where(low, b, a), COLS - step)
             if swap:
                 ref[e, :C] = down
                 ref[e, C : 2 * C] = a
                 ref[e, 2 * C :] = up
             else:
                 ref[e, :C, :COLS] = up
-                ref[e, :C, COLS:] = jnp.where(low, a_up, b_up)
+                ref[e, :C, COLS:] = turn(jnp.where(high, a, b), step)
                 ref[e, C : 2 * C, :COLS] = a
                 ref[e, C : 2 * C, COLS:] = b
                 ref[e, 2 * C :, :COLS] = down
-                ref[e, 2 * C :, COLS:] = jnp.where(high, a_down, b_down)
-
-    def assemble(e, k, s, x, ur):
-        fl, fr = from_left[k], from_right[k]
-        keep = row_mask(e)
-        ui = jnp.broadcast_to(ur, (C, COLS)) * keep
-        main = x + (ui + own_u * keep)
-        side = jnp.where(
-            lane < HALO, turn(fr, -16 * s),
-            jnp.where(lane >= COLS - HALO, turn(fl, 112 - 16 * s), 0.0),
-        )
-        side = side + (ui * side_mask + side_u * keep)
+                ref[e, 2 * C :, COLS:] = turn(jnp.where(low, a, b), COLS - step)
+
+    lower = lane % 32 < 16
+    for k in range(EXT // 8):
+        fl, fr = partners(col_even, col_a, col_b, k)
+        merged[0, k] = jnp.where(lower, fl, turn(fr, 16))
+        merged[1, k] = jnp.where(lower, turn(fl, -16), fr)
+    near_sides = (lane < HALO) | (lane >= COLS - HALO)
+    one_hot = jnp.where(
+        lax.broadcasted_iota(jnp.int32, (COLS, 8 * COLS), 0)
+        == lax.broadcasted_iota(jnp.int32, (COLS, 8 * COLS), 1) // COLS, 1.0, 0.0,
+    ).astype(BF16)
+
+    def fanned(values):
+        both = dot(jnp.concatenate(split(values), axis=0), one_hot)
+        return both[:C] + both[C:]
+
+    def assemble(e, k, s, x, ui, keep):
+        side = turn(merged[s % 2, k], -16 * s if s % 2 else -16 * s - 16)
+        sides[e] = side
+        side = jnp.where(near_sides, side, 0.0)
+        u_main, u_side = ui + own_u, ui * side_mask + side_u
+        if keep is not None:
+            u_main, u_side = u_main * keep, u_side * keep
+        main = x + u_main
+        side = side + u_side
         x0[e, :, :COLS] = main
         x0[e, :, COLS:] = side
         put_shifted(xh, xl, e, main, side, d0, False)
 
-    def assemble_g(f, k, s, g):
-        gm[f] = g
-        gb[f] = jnp.where(
-            lane < GHALO, turn(from_right[k], -(16 * s + 12)),
-            jnp.where(lane >= COLS - GHALO, turn(from_left[k], 124 - 16 * s), 0.0),
-        )
-
-    for e in tuple(range(HALO)) + tuple(range(HALO + ROWS, EXT)):
-        where_, at = source(e)
-        ref = above if where_ == 0 else below
-        assemble(e, e // 8, e % 8, ref[at], row_u[:, e : e + 1])
-        if 8 <= e < HALO:
-            assemble_g(e - 8, e // 8, e % 8, above[HALO + e - 8])
-        if HALO + ROWS <= e < HALO + ROWS + GHALO:
-            assemble_g(e - 8, e // 8, e % 8, below[HALO + at])
+    fan_low = fanned(row_u), fanned(turn(row_u, -8))
+    fan_high = fanned(turn(row_u, -(HALO + ROWS))), fanned(turn(row_u, -(HALO + ROWS + 8)))
+    for at in range(HALO):
+        above, below = partners(row_even, row_a, row_b, at)
+        e, f = at, at + HALO + ROWS
+        part = slice((at % 8) * COLS, (at % 8 + 1) * COLS)
+        assemble(e, e // 8, e % 8, above, fan_low[at // 8][:, part], row_mask(e))
+        assemble(f, f // 8, f % 8, below, fan_high[at // 8][:, part], row_mask(f))
 
     def assemble_own(q, carry):
-        ur = turn(row_u, (COLS - HALO - 8 * q) % COLS)
+        fan = fanned(turn(row_u, (COLS - HALO - 8 * q) % COLS))
         for s in range(8):
             k, slot = q + 1 + (s + 4) // 8, (s + 4) % 8
             at = 8 * q + s
-            assemble(at + HALO, k, slot, pair[pl.ds(at, C, stride=ROWS), :], ur[:, s : s + 1])
-            assemble_g(at + GHALO, k, slot, cot[pl.ds(at, C, stride=ROWS), :])
+            assemble(
+                at + HALO, k, slot, pair[pl.ds(at, C, stride=ROWS), :], fan[:, s * COLS : (s + 1) * COLS], None
+            )
         return carry
 
     lax.fori_loop(0, ROWS // 8, assemble_own, 0)
@@ -253,7 +261,18 @@
         if own:
             pair_out[pl.ds(e - HALO, C, stride=ROWS), :] = x0[e, :, :COLS] + t[:, :COLS]
         slope = 1.0 - t * t
-        put_shifted(sh, sl, e - 8, gm[e - 8] * slope[:, :COLS], gb[e - 8] * slope[:, COLS:], d1, True)
+        if own:
+            g = cot[pl.ds(e - HALO, C, stride=ROWS), :]
+            gm[e - HALO] = g
+        elif e < HALO:
+            g = partners(row_even, row_a, row_b, HALO + e - 8)[0]
+        else:
+            g = partners(row_even, row_a, row_b, e - ROWS)[1]
+        side = sides[e]
+        g_side = jnp.where(
+            lane < GHALO, turn(side, -12), jnp.where(lane >= COLS - GHALO, turn(side, 12), 0.0)
+        )
+        put_shifted(sh, sl, e - 8, g * slope[:, :COLS], g_side * slope[:, COLS:], d1, True)
 
     def second_own(i, carry):
         second(i + HALO, True)
@@ -274,7 +293,7 @@
         )
         for k in range(2):
             at = 2 * i + k
-            g1 = gm[at + GHALO] + acc[:, k * COLS : (k + 1) * COLS]
+            g1 = gm[at] + acc[:, k * COLS : (k + 1) * COLS]
             t = t0s[at + HALO]
             g1s[at] = g1
             s0s[at] = g1 * (1.0 - t * t)
@@ -330,7 +349,7 @@
     send[...] = buf[1 : PEERS + 1]
 
 
-def layers(dilation, pair, cot, above, below, from_left, from_right, fields, wts):
+def layers(dilation, pair, cot, row_a, row_b, col_a, col_b, fields, wts):
     return pl.pallas_call(
         main_kernel,
         in_specs=[SMEM] + [VMEM] * 8,
@@ -347,8 +366,9 @@
             pltpu.VMEM((EXT, 3 * C, 2 * COLS), BF16),
             pltpu.VMEM((GEXT, 3 * C, COLS), BF16),
             pltpu.VMEM((GEXT, 3 * C, COLS), BF16),
-            pltpu.VMEM((GEXT, C, COLS), F32),
-            pltpu.VMEM((GEXT, C, COLS), F32),
+            pltpu.VMEM((ROWS, C, COLS), F32),
+            pltpu.VMEM((EXT, C, COLS), F32),
+            pltpu.VMEM((2, EXT // 8, C, COLS), F32),
             pltpu.VMEM((EXT, C, COLS), F32),
             pltpu.VMEM((ROWS, C, COLS), F32),
             pltpu.VMEM((ROWS, C, COLS), F32),
@@ -356,7 +376,7 @@
         ],
         compiler_params=pltpu.CompilerParams(vmem_limit_bytes=40 * 2**20),
         name="layers",
-    )(dilation, pair, cot, above, below, from_left, from_right, fields, wts)
+    )(dilation, pair, cot, row_a, row_b, col_a, col_b, fields, wts)
 
 
 def finish_kernel(parts, proj_t, out):
@@ -374,10 +394,10 @@
 
 def local(embed, proj, pair_in, kernels, dilation, cotangent):
     rows, cols = 32, 8
-    down = [(i, i + 1) for i in range(rows - 1)]
-    up = [(i + 1, i) for i in range(rows - 1)]
-    right = [(i, i + 1) for i in range(cols - 1)]
-    left = [(i + 1, i) for i in range(cols - 1)]
+    row_first = [(i, i ^ 1) for i in range(rows)]
+    row_second = [(i, ((i + 1) ^ 1) - 1) for i in range(1, rows - 1)]
+    col_first = [(i, i ^ 1) for i in range(cols)]
+    col_second = [(i, ((i + 1) ^ 1) - 1) for i in range(1, cols - 1)]
     same_core = [[2 * i + core for i in range(PEERS)] for core in range(2)]
     chips = [[(2 * g + core) * cols + c for core in range(2) for c in range(cols)] for g in range(PEERS)]
     packs = jax.ShapeDtypeStruct((PEERS, C // 2, COLS), F32)
@@ -385,36 +405,34 @@
 
     pair = pair_in.reshape(C * ROWS, COLS)
     cot = cotangent.reshape(C * ROWS, COLS)
-    low_edge, high_edge = pl.pallas_call(
+    edge_a, edge_b = pl.pallas_call(
         edges_kernel, in_specs=[VMEM] * 2, out_specs=[VMEM] * 2,
         out_shape=[jax.ShapeDtypeStruct((HALO + GHALO, C, COLS), F32)] * 2, name="edges",
         compiler_params=pltpu.CompilerParams(vmem_limit_bytes=8 * 2**20),
     )(pair, cot)
-    low_edge, high_edge, embed = lax.optimization_barrier((low_edge, high_edge, embed))
-    above = lax.ppermute(low_edge, "row", down)
-    below = lax.ppermute(high_edge, "row", up)
+    edge_a, edge_b, embed = lax.optimization_barrier((edge_a, edge_b, embed))
+    row_b = lax.ppermute(edge_b, "row", row_second)
+    row_a = lax.ppermute(edge_a, "row", row_first)
 
     parts = pl.pallas_call(
         project_kernel, in_specs=[VMEM, VMEM], out_specs=VMEM, out_shape=packs, name="project",
     )(embed, proj_t)
     parts = lax.all_to_all(parts, ("row", "col"), 0, 0, tiled=True, axis_index_groups=chips)
 
-    to_left, to_right = pl.pallas_call(
+    strip_a, strip_b = pl.pallas_call(
         strips_kernel,
         in_specs=[VMEM] * 4,
         out_specs=[VMEM] * 2,
         out_shape=[jax.ShapeDtypeStruct((EXT // 8, C, COLS), F32)] * 2,
         compiler_params=pltpu.CompilerParams(vmem_limit_bytes=8 * 2**20),
         name="strips",
-    )(pair, cot, above, below)
-    parts, to_left, to_right = lax.optimization_barrier((parts, to_left, to_right))
-    from_left = lax.ppermute(to_right, "col", right)
-    from_right = lax.ppermute(to_left, "col", left)
-
-    fields = pl.pallas_call(
-        combine_kernel, in_specs=[VMEM], out_specs=VMEM, out_shape=packs, name="combine",
-        cost_estimate=pl.CostEstimate(flops=0, transcendentals=0, bytes_accessed=64 * 2**20),
-    )(parts)
+    )(pair, cot, row_a, row_b)
+    parts, strip_a, strip_b = lax.optimization_barrier((parts, strip_a, strip_b))
+    col_b = lax.ppermute(strip_b, "col", col_second)
+    col_a = lax.ppermute(strip_a, "col", col_first)
+
+    own = jnp.sum(parts, axis=0)
+    fields = jnp.broadcast_to(own, (PEERS,) + own.shape)
     fields = lax.all_to_all(fields, "row", 0, 0, tiled=True, axis_index_groups=same_core)
 
     taps = kernels.transpose(0, 3, 4, 1, 2).reshape(18, C, C)
@@ -422,7 +440,7 @@
         weights_kernel, in_specs=[VMEM], out_specs=VMEM,
         out_shape=jax.ShapeDtypeStruct((4, 2 * C, TAPS), BF16), name="weights",
     )(taps)
-    pair_out, send = layers(dilation, pair, cot, above, below, from_left, from_right, fields, wts)
+    pair_out, send = layers(dilation, pair, cot, row_a, row_b, col_a, col_b, fields, wts)
 
     got = lax.all_to_all(send, "row", 0, 0, tiled=True, axis_index_groups=same_core)
     own = jnp.sum(got, axis=0)

time: 105 us -> 93.8 us (0.89)
  starting transfers between devices: 27 us -> 20.5 us
  Pallas kernels: 29.6 us -> 25.9 us
  blocking collectives: 34.3 us -> 32.6 us
    ppermute x4, starting transfers between devices: 10.3 us -> 6.27 us  [the longest x1 3.33 us: local(): row_a = lax.ppermute(edge_a, 'row', row_first)]
    all_to_all x1, starting transfers between devices: 9.62 us -> 7.42 us  [local(): lax.all_to_all(fields, 'row', 0, 0, tiled=True, axis_index_groups=same_core)]
    pallas_call x1, Pallas kernels: 18.4 us -> 16.3 us  [layers(): pl.pallas_call(main_kernel, in_specs=[SMEM] + [VMEM] * 8, out_specs=[VMEM...]
    all_to_all x1, waiting for transfers between devices: 0.01 us -> 1.96 us  [local(): lax.all_to_all(fields, 'row', 0, 0, tiled=True, axis_index_groups=same_core)]
    all_to_all x1, blocking collectives: 14.5 us -> 12.8 us  [local(): lax.all_to_all(send, 'row', 0, 0, tiled=True, axis_index_groups=same_core)]
    pallas_call x1 -> x0, Pallas kernels: 1.64 us -> none  [local(): pl.pallas_call(combine_kernel, in_specs=[VMEM], out_specs=VMEM, out_shape...]
    ppermute x4, waiting for transfers between devices: 3.57 us -> 2.32 us  [the longest x1 2.31 us: local(): col_a = lax.ppermute(strip_a, 'col', col_first)]
    unnamed x14 -> x12, local copies, waits for them, and re-layouts: 3.94 us -> 3.27 us
  transfers between devices with their start and end apart: 6 -> 6, of which waited for: 2 -> 3; matrix products, arithmetic and copies ran while one was open for 0% -> 0% of each run, Pallas kernels for 7% -> 8%
where the time goes in v2:
time: 93.8 us; the launch traced here: 93.2 us
  blocking collectives  32.6 us (35%)
  Pallas kernels  25.9 us (28%)
  starting transfers between devices  20.5 us (22%)
  waiting for transfers between devices  9.33 us (10%)
  local copies, waits for them, and re-layouts  3.98 us (4%)
    all_to_all x1, blocking collectives, local(): lax.all_to_all(jnp.broadcast_to(own, (PEERS,) + own.shape), ('row', 'col'...  19.8 us
    pallas_call x1, Pallas kernels, layers(): pl.pallas_call(main_kernel, in_specs=[SMEM] + [VMEM] * 8, out_specs=[VMEM...  16.3 us
    all_to_all x1, blocking collectives, local(): lax.all_to_all(send, 'row', 0, 0, tiled=True, axis_index_groups=same_core)  12.8 us
    all_to_all x1, starting transfers between devices, local(): lax.all_to_all(fields, 'row', 0, 0, tiled=True, axis_index_groups=same_core)  7.42 us
    all_to_all x1, starting transfers between devices, local(): lax.all_to_all(parts, ('row', 'col'), 0, 0, tiled=True, axis_index_groups...  6.86 us
    all_to_all x1, waiting for transfers between devices, local(): lax.all_to_all(parts, ('row', 'col'), 0, 0, tiled=True, axis_index_groups...  5.05 us
    pallas_call x1, Pallas kernels, local(): pl.pallas_call(strips_kernel, in_specs=[VMEM] * 4, out_specs=[VMEM] * 2,...  3.45 us
    ppermute x1, starting transfers between devices, local(): row_a = lax.ppermute(edge_a, 'row', row_first)  3.33 us
  transfers between devices with their start and end apart: 6, of which 3 were waited for; matrix products, arithmetic and copies ran while one was open for 0% of the time, Pallas kernels for 8%

profile of v2, /device:TPU:1, one launch (start us, length us, event | category | flops | bytes accessed | tf_op | source)
XLA Modules:
  0.0 93.2 jit_solution(852627011718421344)
XLA Ops:
  0.6 0.0 copy-start
  0.6 1.1 %copy-done = f32[48,32,128]{2,1,0:T(8,128)S(1)} copy-done((f32[48,32,128]{2,1,0:T(8,128)S(1)}, f32[48,32,128]{2,1,0:T(8,128)}, u32[]{:S(2)}) %copy-start) | copy-done | bytes 786456
  1.8 0.0 copy-start.2
  1.8 1.1 %copy-done.2 = f32[48,32,128]{2,1,0:T(8,128)S(1)} copy-done((f32[48,32,128]{2,1,0:T(8,128)S(1)}, f32[48,32,128]{2,1,0:T(8,128)}, u32[]{:S(2)}) %copy-start.2) | copy-done | bytes 786456
  2.9 0.0 copy-start.1
  2.9 0.0 copy-start.3
  2.9 0.4 edges.1
  3.3 3.3 %collective-permute-start = (f32[16,48,128]{2,1,0:T(8,128)S(1)}, f32[16,48,128]{2,1,0:T(8,128)S(1)}, u32[]{:S(2)}, u32[]{:S(2)}) collective-permute-start(f32[16,48,128]{2,1,0:T(8,128)S(1)} %get-tuple-element.16), channel_id=1, source_target_pairs={{0,8},{8,0},{16,24},{24,16},{32,40},{40,32},{48,56},{56,48},{64,72... | collective-permute-start | bytes 1179656 | tf_op jit(solution)/shard_map/ppermute | solution.py:415
  6.7 1.9 %collective-permute-start.1 = (f32[16,48,128]{2,1,0:T(8,128)S(1)}, f32[16,48,128]{2,1,0:T(8,128)S(1)}, u32[]{:S(2)}, u32[]{:S(2)}) collective-permute-start(f32[16,48,128]{2,1,0:T(8,128)S(1)} %get-tuple-element.17), channel_id=1, source_target_pairs={{8,16},{16,8},{24,32},{32,24},{40,48},{48,40},{56,64},{64,56},{72,... | collective-permute-start | bytes 1179656 | tf_op jit(solution)/shard_map/ppermute | solution.py:414
  8.6 1.7 %project.1 = f32[16,24,128]{2,1,0:T(8,128)} custom-call(f32[32,64]{1,0:T(8,128)} %embed, f32[48,64]{1,0:T(8,128)} %bitcast.14), custom_call_target="tpu_custom_call" | custom-call | tf_op jit(solution)/shard_map/project/pallas_call | solution.py:417
  10.3 6.9 %all-to-all-start = ((f32[16,24,128]{2,1,0:T(8,128)}), f32[16,24,128]{2,1,0:T(8,128)S(1)}, u32[]{:S(2)}, u32[]{:S(2)}) async-start(f32[16,24,128]{2,1,0:T(8,128)} %project.1), calls=%async_computation | async-start | bytes 393216 | tf_op jit(solution)/shard_map/all_to_all | solution.py:420
  17.1 0.0 collective-permute-done.got_a.row_a
  17.1 0.0 collective-permute-done.1.got_b.row_b
  17.1 0.0 copy-done.1
  17.1 0.0 copy-done.3
  17.2 3.5 %strips.1 = (f32[7,48,128]{2,1,0:T(8,128)S(1)}, f32[7,48,128]{2,1,0:T(8,128)S(1)}) custom-call(f32[1536,128]{1,0:T(8,128)S(1)} %bitcast.8, f32[1536,128]{1,0:T(8,128)S(1)} %bitcast.11, f32[16,48,128]{2,1,0:T(8,128)S(1)} %collective-permute-done.got_a.row_a, f32[16,48,128]{2,1,0:T(8,128)S(1)} %collective-permute-done.1.got_b.row_b), custom_call_target="tpu_custom_call" | custom-call | tf_op jit(solution)/shard_map/strips/pallas_call | solution.py:422
  20.6 5.1 %all-to-all-done = f32[16,24,128]{2,1,0:T(8,128)S(1)} async-done(((f32[16,24,128]{2,1,0:T(8,128)}), f32[16,24,128]{2,1,0:T(8,128)S(1)}, u32[]{:S(2)}, u32[]{:S(2)}) %all-to-all-start) | async-done | bytes 196640 | tf_op jit(solution)/shard_map/all_to_all | solution.py:420
  25.7 0.7 broadcast_in_dim.6
  26.4 7.4 %all-to-all-start.1 = ((f32[16,24,128]{2,1,0:T(8,128)}), f32[16,24,128]{2,1,0:T(8,128)S(1)}, u32[]{:S(2)}, u32[]{:S(2)}) async-start(f32[16,24,128]{2,1,0:T(8,128)} %broadcast_in_dim.6), calls=%async_computation.1 | async-start | bytes 393216 | tf_op jit(solution)/shard_map/all_to_all | solution.py:436
  33.8 0.4 collective-permute-start.2
  34.2 0.7 collective-permute-start.3
  34.8 0.0 copy-start.5
  34.9 2.1 %weights.1.wts = bf16[4,96,432]{2,1,0:T(8,128)(2,1)} custom-call(f32[18,48,48]{2,1,0:T(8,128)} %bitcast.13), custom_call_target="tpu_custom_call" | custom-call | tf_op jit(solution)/shard_map/weights/pallas_call | solution.py:439
  37.0 2.3 %collective-permute-done.2.col_a = f32[7,48,128]{2,1,0:T(8,128)S(1)} collective-permute-done((f32[7,48,128]{2,1,0:T(8,128)S(1)}, f32[7,48,128]{2,1,0:T(8,128)S(1)}, u32[]{:S(2)}, u32[]{:S(2)}) %collective-permute-start.2) | collective-permute-done | bytes 172064 | tf_op jit(solution)/shard_map/ppermute | solution.py:432
  39.3 0.0 collective-permute-done.3.col_b
  39.3 2.0 %all-to-all-done.1.fields = f32[16,24,128]{2,1,0:T(8,128)S(1)} async-done(((f32[16,24,128]{2,1,0:T(8,128)}), f32[16,24,128]{2,1,0:T(8,128)S(1)}, u32[]{:S(2)}, u32[]{:S(2)}) %all-to-all-start.1) | async-done | bytes 196640 | tf_op jit(solution)/shard_map/all_to_all | solution.py:436
  41.3 0.0 copy-done.5
  41.3 0.0 copy-start.4
  41.3 1.0 %copy-done.4 = bf16[4,96,432]{2,1,0:T(8,128)(2,1)S(1)} copy-done((bf16[4,96,432]{2,1,0:T(8,128)(2,1)S(1)}, bf16[4,96,432]{2,1,0:T(8,128)(2,1)}, u32[]{:S(2)}) %copy-start.4) | copy-done | bytes 331800
  42.3 16.3 %layers.1 = (f32[1536,128]{1,0:T(8,128)}, f32[16,24,128]{2,1,0:T(8,128)S(1)}) custom-call(s32[2]{0:T(128)S(1)} %copy-done.5, f32[1536,128]{1,0:T(8,128)S(1)} %bitcast.9, f32[1536,128]{1,0:T(8,128)S(1)} %bitcast.12, f32[16,48,128]{2,1,0:T(8,128)S(1)} %collective-permute-done.got_a.row_a, f32[16,48,128]{2,1,0:T(8,128)S(1)} %collective-permute-done.1.got_b.row_b, ...), custom_call_target="tpu_custom_call" | custom-call | tf_op jit(solution)/shard_map/layers/pallas_call | solution.py:353
  58.6 12.8 %all_to_all.20 = f32[16,24,128]{2,1,0:T(8,128)S(1)} all-to-all(f32[16,24,128]{2,1,0:T(8,128)S(1)} %get-tuple-element.25), channel_id=1, replica_groups={{0,16,32,48,64,80,96,112,128,144,160,176,192,208,224,240},{8,24,40,56,7..., dimensions={0} | all-to-all | bytes 393216 | tf_op jit(solution)/shard_map/all_to_all | solution.py:445
  71.5 19.8 %all_to_all.21.parts = f32[16,24,128]{2,1,0:T(8,128)} all-to-all(f32[16,24,128]{2,1,0:T(8,128)S(1)} %broadcast_in_dim.7), channel_id=1, replica_groups={{0,1,2,3,4,5,6,7,8,9,10,11,12,13,14,15},{16,17,18,19,20,21,22,23,24,25,..., dimensions={0} | all-to-all | bytes 393216 | tf_op jit(solution)/shard_map/all_to_all | solution.py:447
  91.3 1.9 %finish.1 = f32[32,64]{1,0:T(8,128)} custom-call(f32[16,24,128]{2,1,0:T(8,128)} %all_to_all.21.parts, f32[48,64]{1,0:T(8,128)} %bitcast.15), custom_call_target="tpu_custom_call" | custom-call | tf_op jit(solution)/shard_map/finish/pallas_call | solution.py:450
  (3 shorter events, 0.1 us)
Async XLA Ops:
  0.6 1.1 %copy-start = (f32[48,32,128]{2,1,0:T(8,128)S(1)}, f32[48,32,128]{2,1,0:T(8,128)}, u32[]{:S(2)}) copy-start(f32[48,32,128]{2,1,0:T(8,128)} %param.8) | copy-start | bytes 2359300
  1.8 1.1 %copy-start.2 = (f32[48,32,128]{2,1,0:T(8,128)S(1)}, f32[48,32,128]{2,1,0:T(8,128)}, u32[]{:S(2)}) copy-start(f32[48,32,128]{2,1,0:T(8,128)} %param.11) | copy-start | bytes 2359300
  2.9 14.2 %copy-start.1 = (f32[48,32,128]{2,1,0:T(8,128)S(1)}, f32[48,32,128]{2,1,0:T(8,128)}, u32[]{:S(2)}) copy-start(f32[48,32,128]{2,1,0:T(8,128)} %param.8) | copy-start | bytes 2359300
  2.9 14.2 %copy-start.3 = (f32[48,32,128]{2,1,0:T(8,128)S(1)}, f32[48,32,128]{2,1,0:T(8,128)}, u32[]{:S(2)}) copy-start(f32[48,32,128]{2,1,0:T(8,128)} %param.11) | copy-start | bytes 2359300
  3.3 13.8 %collective-permute-start = (f32[16,48,128]{2,1,0:T(8,128)S(1)}, f32[16,48,128]{2,1,0:T(8,128)S(1)}, u32[]{:S(2)}, u32[]{:S(2)}) collective-permute-start(f32[16,48,128]{2,1,0:T(8,128)S(1)} %get-tuple-element.16), channel_id=1, source_target_pairs={{0,8},{8,0},{16,24},{24,16},{32,40},{40,32},{48,56},{56,48},{64,72... | collective-permute-start | bytes 1179656 | tf_op jit(solution)/shard_map/ppermute | solution.py:415
  6.7 10.5 %collective-permute-start.1 = (f32[16,48,128]{2,1,0:T(8,128)S(1)}, f32[16,48,128]{2,1,0:T(8,128)S(1)}, u32[]{:S(2)}, u32[]{:S(2)}) collective-permute-start(f32[16,48,128]{2,1,0:T(8,128)S(1)} %get-tuple-element.17), channel_id=1, source_target_pairs={{8,16},{16,8},{24,32},{32,24},{40,48},{48,40},{56,64},{64,56},{72,... | collective-permute-start | bytes 1179656 | tf_op jit(solution)/shard_map/ppermute | solution.py:414
  10.3 15.4 %all-to-all-start = ((f32[16,24,128]{2,1,0:T(8,128)}), f32[16,24,128]{2,1,0:T(8,128)S(1)}, u32[]{:S(2)}, u32[]{:S(2)}) async-start(f32[16,24,128]{2,1,0:T(8,128)} %project.1), calls=%async_computation | async-start | bytes 393216 | tf_op jit(solution)/shard_map/all_to_all | solution.py:420
  26.4 14.9 %all-to-all-start.1 = ((f32[16,24,128]{2,1,0:T(8,128)}), f32[16,24,128]{2,1,0:T(8,128)S(1)}, u32[]{:S(2)}, u32[]{:S(2)}) async-start(f32[16,24,128]{2,1,0:T(8,128)} %broadcast_in_dim.6), calls=%async_computation.1 | async-start | bytes 393216 | tf_op jit(solution)/shard_map/all_to_all | solution.py:436
  33.8 5.5 %collective-permute-start.2 = (f32[7,48,128]{2,1,0:T(8,128)S(1)}, f32[7,48,128]{2,1,0:T(8,128)S(1)}, u32[]{:S(2)}, u32[]{:S(2)}) collective-permute-start(f32[7,48,128]{2,1,0:T(8,128)S(1)} %get-tuple-element.21), channel_id=1, source_target_pairs={{0,1},{1,0},{2,3},{3,2},{4,5},{5,4},{6,7},{7,6},{8,9},{9,8},{10,11... | collective-permute-start | bytes 516104 | tf_op jit(solution)/shard_map/ppermute | solution.py:432
  34.2 5.1 %collective-permute-start.3 = (f32[7,48,128]{2,1,0:T(8,128)S(1)}, f32[7,48,128]{2,1,0:T(8,128)S(1)}, u32[]{:S(2)}, u32[]{:S(2)}) collective-permute-start(f32[7,48,128]{2,1,0:T(8,128)S(1)} %get-tuple-element.22), channel_id=1, source_target_pairs={{1,2},{2,1},{3,4},{4,3},{5,6},{6,5},{9,10},{10,9},{11,12},{12,11},... | collective-permute-start | bytes 516104 | tf_op jit(solution)/shard_map/ppermute | solution.py:431
  34.8 6.4 %copy-start.5 = (s32[2]{0:T(128)S(1)}, s32[2]{0:T(128)}, u32[]{:S(2)}) copy-start(s32[2]{0:T(128)} %dil.1) | copy-start | bytes 28
  41.3 1.0 %copy-start.4 = (bf16[4,96,432]{2,1,0:T(8,128)(2,1)S(1)}, bf16[4,96,432]{2,1,0:T(8,128)(2,1)}, u32[]{:S(2)}) copy-start(bf16[4,96,432]{2,1,0:T(8,128)(2,1)} %weights.1.wts) | copy-start | bytes 995332

commit v3 on v2

--- a/solution.py
+++ b/solution.py
@@ -21,6 +21,7 @@
 BF16 = jnp.bfloat16
 VMEM = pl.BlockSpec(memory_space=pltpu.VMEM)
 SMEM = pl.BlockSpec(memory_space=pltpu.SMEM)
+SMALL = pltpu.CompilerParams(vmem_limit_bytes=4 * 2**20)
 
 
 def lanes_of(rows, width=COLS):
@@ -51,8 +52,19 @@
     return first, second
 
 
-def project_kernel(embed, proj_t, out):
-    core = lax.axis_index("row") % 2
+def open_kernel(embed_hbm, proj_hbm, pair_hbm, cot_hbm, out, to_a, to_b, embed, proj_t, pair, cot, sems):
+    copies = [
+        pltpu.make_async_copy(source_, target, sems.at[n])
+        for n, (source_, target) in enumerate(
+            ((embed_hbm, embed), (proj_hbm, proj_t), (pair_hbm, pair), (cot_hbm, cot))
+        )
+    ]
+    for copy in copies:
+        copy.start()
+    row = lax.axis_index("row")
+    core = row % 2
+    copies[0].wait()
+    copies[1].wait()
     part = lax.dot_general(
         proj_t[...], embed[...], (((1,), (1,)), ((), ())),
         precision=lax.Precision.HIGHEST, preferred_element_type=F32,
@@ -61,6 +73,14 @@
     mine = turn(part[: C // 2], 32 * core) + turn(part[C // 2 :], 64 + 32 * core)
     for peer in range(PEERS):
         out[peer] = mine
+    even = core == 0
+    for copy, ref, count, start in ((copies[2], pair, HALO, 0), (copies[3], cot, GHALO, HALO)):
+        copy.wait()
+        for e in range(count):
+            low = ref[pl.ds(e + ROWS - count, C, stride=ROWS), :]
+            high = ref[pl.ds(e, C, stride=ROWS), :]
+            to_a[start + e] = jnp.where(even, low, high)
+            to_b[start + e] = jnp.where(even, high, low)
 
 
 def partners(mine_is_even, got_a, got_b, at):
@@ -147,7 +167,7 @@
 
 def main_kernel(
     dil, pair, cot, row_a, row_b, col_a, col_b, fields, wts, pair_out, send,
-    x0, xh, xl, yh, yl, sh, sl, gm, sides, merged, t0s, s0s, g1s, buf,
+    x0, xh, xl, yh, yl, sh, sl, gm, sides, merged, t0s, s0s, g1s, buf, kept, sem,
 ):
     d0, d1 = dil[0], dil[1]
     row, col = lax.axis_index("row"), lax.axis_index("col")
@@ -251,7 +271,7 @@
         put_shifted(yh, yl, e, main, side, d1, False)
         return carry
 
-    lax.fori_loop(0, EXT - 8, first, 0, unroll=16)
+    lax.fori_loop(0, EXT - 8, first, 0, unroll=48)
 
     def second(e, own):
         acc = weighted(
@@ -259,7 +279,7 @@
         )
         t = jnp.tanh(acc)
         if own:
-            pair_out[pl.ds(e - HALO, C, stride=ROWS), :] = x0[e, :, :COLS] + t[:, :COLS]
+            kept[pl.ds(e - HALO, C, stride=ROWS), :] = x0[e, :, :COLS] + t[:, :COLS]
         slope = 1.0 - t * t
         if own:
             g = cot[pl.ds(e - HALO, C, stride=ROWS), :]
@@ -280,7 +300,10 @@
 
     for e in (8, 9, 10, 11, 44, 45, 46, 47):
         second(e, False)
-    lax.fori_loop(0, ROWS, second_own, 0, unroll=16)
+    lax.fori_loop(0, ROWS, second_own, 0, unroll=32)
+
+    copy = pltpu.make_async_copy(kept, pair_out, sem)
+    copy.start()
 
     def third(i, carry):
         parts_hi, parts_lo = [], []
@@ -299,7 +322,7 @@
             s0s[at] = g1 * (1.0 - t * t)
         return carry
 
-    lax.fori_loop(0, ROWS // 2, third, 0, unroll=8)
+    lax.fori_loop(0, ROWS // 2, third, 0, unroll=16)
 
     lane8 = lanes_of(8)
     edge = ((lane8 < d0) & (col == 0)) | ((lane8 >= COLS - d0) & (col == 7))
@@ -347,13 +370,14 @@
     add(2 * col + 3, 2 * col, made[:, COLS : 2 * COLS])
     add(group + core, group + core + 1, turn(rg + made[:, 2 * COLS :], 64 - 32 * core))
     send[...] = buf[1 : PEERS + 1]
+    copy.wait()
 
 
 def layers(dilation, pair, cot, row_a, row_b, col_a, col_b, fields, wts):
     return pl.pallas_call(
         main_kernel,
         in_specs=[SMEM] + [VMEM] * 8,
-        out_specs=[VMEM] * 2,
+        out_specs=[pl.BlockSpec(memory_space=pl.ANY), VMEM],
         out_shape=[
             jax.ShapeDtypeStruct((C * ROWS, COLS), F32),
             jax.ShapeDtypeStruct((PEERS, C // 2, COLS), F32),
@@ -373,8 +397,10 @@
             pltpu.VMEM((ROWS, C, COLS), F32),
             pltpu.VMEM((ROWS, C, COLS), F32),
             pltpu.VMEM((PEERS + 2, C // 2, COLS), F32),
+            pltpu.VMEM((C * ROWS, COLS), F32),
+            pltpu.SemaphoreType.DMA,
         ],
-        compiler_params=pltpu.CompilerParams(vmem_limit_bytes=40 * 2**20),
+        compiler_params=pltpu.CompilerParams(vmem_limit_bytes=36 * 2**20),
         name="layers",
     )(dilation, pair, cot, row_a, row_b, col_a, col_b, fields, wts)
 
@@ -405,18 +431,22 @@
 
     pair = pair_in.reshape(C * ROWS, COLS)
     cot = cotangent.reshape(C * ROWS, COLS)
-    edge_a, edge_b = pl.pallas_call(
-        edges_kernel, in_specs=[VMEM] * 2, out_specs=[VMEM] * 2,
-        out_shape=[jax.ShapeDtypeStruct((HALO + GHALO, C, COLS), F32)] * 2, name="edges",
-        compiler_params=pltpu.CompilerParams(vmem_limit_bytes=8 * 2**20),
-    )(pair, cot)
-    edge_a, edge_b, embed = lax.optimization_barrier((edge_a, edge_b, embed))
+    any_space = pl.BlockSpec(memory_space=pltpu.HBM)
+    edge = jax.ShapeDtypeStruct((HALO + GHALO, C, COLS), F32)
+    parts, edge_a, edge_b = pl.pallas_call(
+        open_kernel, in_specs=[any_space] * 4, out_specs=[VMEM] * 3, out_shape=[packs, edge, edge],
+        scratch_shapes=[
+            pltpu.VMEM((ROWS, 64), F32),
+            pltpu.VMEM((C, 64), F32),
+            pltpu.VMEM((C * ROWS, COLS), F32),
+            pltpu.VMEM((C * ROWS, COLS), F32),
+            pltpu.SemaphoreType.DMA((4,)),
+        ],
+        compiler_params=pltpu.CompilerParams(vmem_limit_bytes=60 * 2**20), name="open",
+    )(embed, proj_t, pair, cot)
     row_b = lax.ppermute(edge_b, "row", row_second)
     row_a = lax.ppermute(edge_a, "row", row_first)
 
-    parts = pl.pallas_call(
-        project_kernel, in_specs=[VMEM, VMEM], out_specs=VMEM, out_shape=packs, name="project",
-    )(embed, proj_t)
     parts = lax.all_to_all(parts, ("row", "col"), 0, 0, tiled=True, axis_index_groups=chips)
 
     strip_a, strip_b = pl.pallas_call(
@@ -424,22 +454,23 @@
         in_specs=[VMEM] * 4,
         out_specs=[VMEM] * 2,
         out_shape=[jax.ShapeDtypeStruct((EXT // 8, C, COLS), F32)] * 2,
-        compiler_params=pltpu.CompilerParams(vmem_limit_bytes=8 * 2**20),
+        compiler_params=SMALL,
         name="strips",
     )(pair, cot, row_a, row_b)
-    parts, strip_a, strip_b = lax.optimization_barrier((parts, strip_a, strip_b))
-    col_b = lax.ppermute(strip_b, "col", col_second)
-    col_a = lax.ppermute(strip_a, "col", col_first)
-
-    own = jnp.sum(parts, axis=0)
-    fields = jnp.broadcast_to(own, (PEERS,) + own.shape)
-    fields = lax.all_to_all(fields, "row", 0, 0, tiled=True, axis_index_groups=same_core)
-
     taps = kernels.transpose(0, 3, 4, 1, 2).reshape(18, C, C)
     wts = pl.pallas_call(
         weights_kernel, in_specs=[VMEM], out_specs=VMEM,
         out_shape=jax.ShapeDtypeStruct((4, 2 * C, TAPS), BF16), name="weights",
+        compiler_params=SMALL,
     )(taps)
+    parts, strip_a, strip_b, wts = lax.optimization_barrier((parts, strip_a, strip_b, wts))
+    col_b = lax.ppermute(strip_b, "col", col_second)
+    col_a = lax.ppermute(strip_a, "col", col_first)
+
+    own = jnp.sum(parts, axis=0)
+    fields = jnp.broadcast_to(own, (PEERS,) + own.shape)
+    fields = lax.all_to_all(fields, "row", 0, 0, tiled=True, axis_index_groups=same_core)
+
     pair_out, send = layers(dilation, pair, cot, row_a, row_b, col_a, col_b, fields, wts)
 
     got = lax.all_to_all(send, "row", 0, 0, tiled=True, axis_index_groups=same_core)
@@ -450,6 +481,7 @@
     embed_grad = pl.pallas_call(
         finish_kernel, in_specs=[VMEM, VMEM], out_specs=VMEM,
         out_shape=jax.ShapeDtypeStruct((ROWS, 64), F32), name="finish",
+        compiler_params=SMALL,
     )(got, proj_t)
     return (pair_out.reshape(C, ROWS, COLS), embed_grad)
 

time: 93.8 us -> 89.8 us (0.957)
  local copies, waits for them, and re-layouts: 3.98 us -> 0.73 us
  Pallas kernels: 25.9 us -> 23.1 us
  waiting for transfers between devices: 9.33 us -> 11.4 us
    unnamed x12 -> x10, local copies, waits for them, and re-layouts: 3.27 us -> 0.02 us
    ppermute x1, waiting for transfers between devices: 2.31 us -> 4.5 us  [local(): col_a = lax.ppermute(strip_a, 'col', col_first)]
    pallas_call x1, Pallas kernels: 2.14 us -> 0.38 us  [local(): pl.pallas_call(weights_kernel, in_specs=[VMEM], out_specs=VMEM, out_shape...]
    all_to_all x1, starting transfers between devices: 7.42 us -> 6.47 us  [local(): lax.all_to_all(fields, 'row', 0, 0, tiled=True, axis_index_groups=same_core)]
    pallas_call x3 -> x2, Pallas kernels: 18.5 us -> 17.6 us  [the longest x1 15 us: layers(): pl.pallas_call(main_kernel, in_specs=[SMEM] + [VMEM] * 8, out_specs=[pl.B...]
  transfers between devices with their start and end apart: 6 -> 6, of which waited for: 3 -> 3; matrix products, arithmetic and copies ran while one was open for 0% -> 0% of each run, Pallas kernels for 8% -> 5%
where the time goes in v3:
time: 89.8 us; the launch traced here: 89.4 us
  blocking collectives  32.5 us (36%)
  Pallas kernels  23.1 us (26%)
  starting transfers between devices  19.9 us (22%)
  waiting for transfers between devices  11.4 us (13%)
  other arithmetic  0.97 us (1%)
    all_to_all x1, blocking collectives, local(): lax.all_to_all(jnp.broadcast_to(own, (PEERS,) + own.shape), ('row', 'col'...  19.7 us
    pallas_call x1, Pallas kernels, layers(): pl.pallas_call(main_kernel, in_specs=[SMEM] + [VMEM] * 8, out_specs=[pl.B...  15 us
    all_to_all x1, blocking collectives, local(): lax.all_to_all(send, 'row', 0, 0, tiled=True, axis_index_groups=same_core)  12.8 us
    all_to_all x1, starting transfers between devices, local(): lax.all_to_all(parts, ('row', 'col'), 0, 0, tiled=True, axis_index_groups...  7 us
    all_to_all x1, starting transfers between devices, local(): lax.all_to_all(fields, 'row', 0, 0, tiled=True, axis_index_groups=same_core)  6.47 us
    all_to_all x1, waiting for transfers between devices, local(): lax.all_to_all(parts, ('row', 'col'), 0, 0, tiled=True, axis_index_groups...  5.18 us
    ppermute x1, waiting for transfers between devices, local(): col_a = lax.ppermute(strip_a, 'col', col_first)  4.5 us
    pallas_call x1, Pallas kernels, local(): pl.pallas_call(strips_kernel, in_specs=[VMEM] * 4, out_specs=[VMEM] * 2,...  4.13 us
  transfers between devices with their start and end apart: 6, of which 3 were waited for; matrix products, arithmetic and copies ran while one was open for 0% of the time, Pallas kernels for 5%

profile of v3, /device:TPU:1, one launch (start us, length us, event | category | flops | bytes accessed | tf_op | source)
XLA Modules:
  0.0 89.4 jit_solution(3928879451628932642)
XLA Ops:
  0.6 0.0 copy-start.2
  0.6 0.0 copy-start.1
  0.6 2.6 %open.1 = (f32[16,24,128]{2,1,0:T(8,128)}, f32[16,48,128]{2,1,0:T(8,128)}, f32[16,48,128]{2,1,0:T(8,128)}) custom-call(f32[32,64]{1,0:T(8,128)} %embed_hbm.1, f32[48,64]{1,0:T(8,128)} %bitcast.14, f32[1536,128]{1,0:T(8,128)} %bitcast.7, f32[1536,128]{1,0:T(8,128)} %bitcast.10), custom_call_target="tpu_custom_call" | custom-call | tf_op jit(solution)/shard_map/open/pallas_call | solution.py:436
  3.3 0.0 copy-start
  3.3 3.3 %collective-permute-start = (f32[16,48,128]{2,1,0:T(8,128)}, f32[16,48,128]{2,1,0:T(8,128)S(1)}, u32[]{:S(2)}, u32[]{:S(2)}) collective-permute-start(f32[16,48,128]{2,1,0:T(8,128)} %get-tuple-element.13), channel_id=1, source_target_pairs={{0,8},{8,0},{16,24},{24,16},{32,40},{40,32},{48,56},{56,48},{64,72... | collective-permute-start | bytes 1179656 | tf_op jit(solution)/shard_map/ppermute | solution.py:448
  6.6 1.9 %collective-permute-start.1 = (f32[16,48,128]{2,1,0:T(8,128)}, f32[16,48,128]{2,1,0:T(8,128)S(1)}, u32[]{:S(2)}, u32[]{:S(2)}) collective-permute-start(f32[16,48,128]{2,1,0:T(8,128)} %get-tuple-element.14), channel_id=1, source_target_pairs={{8,16},{16,8},{24,32},{32,24},{40,48},{48,40},{56,64},{64,56},{72,... | collective-permute-start | bytes 1179656 | tf_op jit(solution)/shard_map/ppermute | solution.py:447
  8.5 7.0 %all-to-all-start = ((f32[16,24,128]{2,1,0:T(8,128)}), f32[16,24,128]{2,1,0:T(8,128)}, u32[]{:S(2)}, u32[]{:S(2)}) async-start(f32[16,24,128]{2,1,0:T(8,128)} %get-tuple-element.15), calls=%async_computation | async-start | bytes 393216 | tf_op jit(solution)/shard_map/all_to_all | solution.py:450
  15.5 0.0 copy-done.2
  15.5 0.4 weights.1.wts
  15.9 0.0 collective-permute-done.got_a.row_a
  15.9 0.0 collective-permute-done.1.got_b.row_b
  15.9 0.0 copy-done.1
  16.0 0.0 copy-done
  16.0 4.1 %strips.1 = (f32[7,48,128]{2,1,0:T(8,128)}, f32[7,48,128]{2,1,0:T(8,128)S(1)}) custom-call(f32[1536,128]{1,0:T(8,128)S(1)} %bitcast.8, f32[1536,128]{1,0:T(8,128)S(1)} %bitcast.11, f32[16,48,128]{2,1,0:T(8,128)S(1)} %collective-permute-done.got_a.row_a, f32[16,48,128]{2,1,0:T(8,128)S(1)} %collective-permute-done.1.got_b.row_b), custom_call_target="tpu_custom_call" | custom-call | tf_op jit(solution)/shard_map/strips/pallas_call | solution.py:452
  20.1 5.2 %all-to-all-done = f32[16,24,128]{2,1,0:T(8,128)} async-done(((f32[16,24,128]{2,1,0:T(8,128)}), f32[16,24,128]{2,1,0:T(8,128)}, u32[]{:S(2)}, u32[]{:S(2)}) %all-to-all-start) | async-done | bytes 196640 | tf_op jit(solution)/shard_map/all_to_all | solution.py:450
  25.3 0.9 %reduce_sum.18 = f32[24,128]{1,0:T(8,128)S(1)} reduce(f32[16,24,128]{2,1,0:T(8,128)} %all-to-all-done, f32[]{:T(128)} %constant.0.clone.1), dimensions={0}, to_apply=%region_0.0 | reduce | flops 46080 | bytes 208900 | tf_op jit(solution)/shard_map/reduce_sum | solution.py:470
  26.2 0.7 broadcast_in_dim.6
  26.9 0.0 copy-start.4
  26.9 6.5 %all-to-all-start.1 = ((f32[16,24,128]{2,1,0:T(8,128)}), f32[16,24,128]{2,1,0:T(8,128)S(1)}, u32[]{:S(2)}, u32[]{:S(2)}) async-start(f32[16,24,128]{2,1,0:T(8,128)} %broadcast_in_dim.6), calls=%async_computation.1 | async-start | bytes 393216 | tf_op jit(solution)/shard_map/all_to_all | solution.py:472
  33.4 0.4 collective-permute-start.2
  33.8 0.8 collective-permute-start.3
  34.6 4.5 %collective-permute-done.2.col_a = f32[7,48,128]{2,1,0:T(8,128)S(1)} collective-permute-done((f32[7,48,128]{2,1,0:T(8,128)}, f32[7,48,128]{2,1,0:T(8,128)S(1)}, u32[]{:S(2)}, u32[]{:S(2)}) %collective-permute-start.2) | collective-permute-done | bytes 172064 | tf_op jit(solution)/shard_map/ppermute | solution.py:468
  39.1 0.0 collective-permute-done.3.col_b
  39.1 1.8 %all-to-all-done.1.fields = f32[16,24,128]{2,1,0:T(8,128)S(1)} async-done(((f32[16,24,128]{2,1,0:T(8,128)}), f32[16,24,128]{2,1,0:T(8,128)S(1)}, u32[]{:S(2)}, u32[]{:S(2)}) %all-to-all-start.1) | async-done | bytes 196640 | tf_op jit(solution)/shard_map/all_to_all | solution.py:472
  40.9 0.0 copy-done.4
  40.9 15.0 %layers.1 = (f32[1536,128]{1,0:T(8,128)}, f32[16,24,128]{2,1,0:T(8,128)S(1)}) custom-call(s32[2]{0:T(128)S(1)} %copy-done.4, f32[1536,128]{1,0:T(8,128)S(1)} %bitcast.9, f32[1536,128]{1,0:T(8,128)S(1)} %bitcast.12, f32[16,48,128]{2,1,0:T(8,128)S(1)} %collective-permute-done.got_a.row_a, f32[16,48,128]{2,1,0:T(8,128)S(1)} %collective-permute-done.1.got_b.row_b, ...), custom_call_target="tpu_custom_call" | custom-call | tf_op jit(solution)/shard_map/layers/pallas_call | solution.py:377
  55.9 12.8 %all_to_all.20 = f32[16,24,128]{2,1,0:T(8,128)S(1)} all-to-all(f32[16,24,128]{2,1,0:T(8,128)S(1)} %get-tuple-element.23), channel_id=1, replica_groups={{0,16,32,48,64,80,96,112,128,144,160,176,192,208,224,240},{8,24,40,56,7..., dimensions={0} | all-to-all | bytes 393216 | tf_op jit(solution)/shard_map/all_to_all | solution.py:476
  68.7 0.0 copy-start.3
  68.8 19.7 %all_to_all.21.parts = f32[16,24,128]{2,1,0:T(8,128)S(1)} all-to-all(f32[16,24,128]{2,1,0:T(8,128)S(1)} %broadcast_in_dim.7), channel_id=1, replica_groups={{0,1,2,3,4,5,6,7,8,9,10,11,12,13,14,15},{16,17,18,19,20,21,22,23,24,25,..., dimensions={0} | all-to-all | bytes 393216 | tf_op jit(solution)/shard_map/all_to_all | solution.py:478
  88.5 0.0 copy-done.3
  88.5 0.9 %finish.1 = f32[32,64]{1,0:T(8,128)} custom-call(f32[16,24,128]{2,1,0:T(8,128)S(1)} %all_to_all.21.parts, f32[48,64]{1,0:T(8,128)S(1)} %bitcast.15), custom_call_target="tpu_custom_call" | custom-call | tf_op jit(solution)/shard_map/finish/pallas_call | solution.py:481
  (2 shorter events, 0.0 us)
Async XLA Ops:
  0.6 14.9 %copy-start.2 = (f32[2,48,48,3,3]{2,1,4,3,0:T(8,128)S(1)}, f32[2,48,48,3,3]{2,1,4,3,0:T(8,128)}, u32[]{:S(2)}) copy-start(f32[2,48,48,3,3]{2,1,4,3,0:T(8,128)} %param.9) | copy-start | bytes 497668
  0.6 15.3 %copy-start.1 = (f32[48,32,128]{2,1,0:T(8,128)S(1)}, f32[48,32,128]{2,1,0:T(8,128)}, u32[]{:S(2)}) copy-start(f32[48,32,128]{2,1,0:T(8,128)} %param.11) | copy-start | bytes 2359300
  3.3 12.7 %copy-start = (f32[48,32,128]{2,1,0:T(8,128)S(1)}, f32[48,32,128]{2,1,0:T(8,128)}, u32[]{:S(2)}) copy-start(f32[48,32,128]{2,1,0:T(8,128)} %param.8) | copy-start | bytes 2359300
  3.3 12.6 %collective-permute-start = (f32[16,48,128]{2,1,0:T(8,128)}, f32[16,48,128]{2,1,0:T(8,128)S(1)}, u32[]{:S(2)}, u32[]{:S(2)}) collective-permute-start(f32[16,48,128]{2,1,0:T(8,128)} %get-tuple-element.13), channel_id=1, source_target_pairs={{0,8},{8,0},{16,24},{24,16},{32,40},{40,32},{48,56},{56,48},{64,72... | collective-permute-start | bytes 1179656 | tf_op jit(solution)/shard_map/ppermute | solution.py:448
  6.6 9.3 %collective-permute-start.1 = (f32[16,48,128]{2,1,0:T(8,128)}, f32[16,48,128]{2,1,0:T(8,128)S(1)}, u32[]{:S(2)}, u32[]{:S(2)}) collective-permute-start(f32[16,48,128]{2,1,0:T(8,128)} %get-tuple-element.14), channel_id=1, source_target_pairs={{8,16},{16,8},{24,32},{32,24},{40,48},{48,40},{56,64},{64,56},{72,... | collective-permute-start | bytes 1179656 | tf_op jit(solution)/shard_map/ppermute | solution.py:447
  8.5 16.7 %all-to-all-start = ((f32[16,24,128]{2,1,0:T(8,128)}), f32[16,24,128]{2,1,0:T(8,128)}, u32[]{:S(2)}, u32[]{:S(2)}) async-start(f32[16,24,128]{2,1,0:T(8,128)} %get-tuple-element.15), calls=%async_computation | async-start | bytes 393216 | tf_op jit(solution)/shard_map/all_to_all | solution.py:450
  26.9 14.0 %copy-start.4 = (s32[2]{0:T(128)S(1)}, s32[2]{0:T(128)}, u32[]{:S(2)}) copy-start(s32[2]{0:T(128)} %dil.1) | copy-start | bytes 28
  26.9 14.0 %all-to-all-start.1 = ((f32[16,24,128]{2,1,0:T(8,128)}), f32[16,24,128]{2,1,0:T(8,128)S(1)}, u32[]{:S(2)}, u32[]{:S(2)}) async-start(f32[16,24,128]{2,1,0:T(8,128)} %broadcast_in_dim.6), calls=%async_computation.1 | async-start | bytes 393216 | tf_op jit(solution)/shard_map/all_to_all | solution.py:472
  33.4 5.7 %collective-permute-start.2 = (f32[7,48,128]{2,1,0:T(8,128)}, f32[7,48,128]{2,1,0:T(8,128)S(1)}, u32[]{:S(2)}, u32[]{:S(2)}) collective-permute-start(f32[7,48,128]{2,1,0:T(8,128)} %get-tuple-element.18), channel_id=1, source_target_pairs={{0,1},{1,0},{2,3},{3,2},{4,5},{5,4},{6,7},{7,6},{8,9},{9,8},{10,11... | collective-permute-start | bytes 516104 | tf_op jit(solution)/shard_map/ppermute | solution.py:468
  33.8 5.3 %collective-permute-start.3 = (f32[7,48,128]{2,1,0:T(8,128)S(1)}, f32[7,48,128]{2,1,0:T(8,128)S(1)}, u32[]{:S(2)}, u32[]{:S(2)}) collective-permute-start(f32[7,48,128]{2,1,0:T(8,128)S(1)} %get-tuple-element.19), channel_id=1, source_target_pairs={{1,2},{2,1},{3,4},{4,3},{5,6},{6,5},{9,10},{10,9},{11,12},{12,11},... | collective-permute-start | bytes 516104 | tf_op jit(solution)/shard_map/ppermute | solution.py:467
  68.7 19.7 %copy-start.3 = (f32[64,48]{0,1:T(8,128)S(1)}, f32[64,48]{0,1:T(8,128)}, u32[]{:S(2)}) copy-start(f32[64,48]{0,1:T(8,128)} %param.7) | copy-start | bytes 36868

commit v4 on v3

--- a/solution.py
+++ b/solution.py
@@ -104,6 +104,14 @@
             high = ref[pl.ds(e, C, stride=ROWS), :]
             to_a[start + e] = jnp.where(even, low, high)
             to_b[start + e] = jnp.where(even, high, low)
+
+
+def combine_kernel(parts, out):
+    total = parts[0]
+    for peer in range(1, PEERS):
+        total = total + parts[peer]
+    for peer in range(PEERS):
+        out[peer] = total
 
 
 def strips_kernel(pair, cot, got_a, got_b, to_a, to_b):
@@ -167,7 +175,7 @@
 
 def main_kernel(
     dil, pair, cot, row_a, row_b, col_a, col_b, fields, wts, pair_out, send,
-    x0, xh, xl, yh, yl, sh, sl, gm, sides, merged, t0s, s0s, g1s, buf, kept, sem,
+    x0, mh, ml, xh, xl, yh, yl, sh, sl, gm, sides, merged, t0s, s0s, g1s, buf, kept, sem,
 ):
     d0, d1 = dil[0], dil[1]
     row, col = lax.axis_index("row"), lax.axis_index("col")
@@ -216,6 +224,19 @@
         == lax.broadcasted_iota(jnp.int32, (COLS, 8 * COLS), 1) // COLS, 1.0, 0.0,
     ).astype(BF16)
 
+    source_lane = lax.broadcasted_iota(jnp.int32, (2 * COLS, 4 * COLS), 0)
+    target_lane = lax.broadcasted_iota(jnp.int32, (2 * COLS, 4 * COLS), 1)
+    wanted = jnp.where(target_lane < 2 * COLS, target_lane - d0, target_lane + d0) & (2 * COLS - 1)
+    shifts = jnp.where(source_lane == wanted, 1.0, 0.0).astype(BF16)
+
+    def shift_rows(e, count):
+        rows = pl.ds(e, count)
+        for middle, ref in ((mh, xh), (ml, xl)):
+            moved = dot(middle[rows].reshape(count * C, 2 * COLS), shifts)
+            moved = moved.astype(BF16).reshape(count, C, 4 * COLS)
+            ref[rows, :C] = moved[:, :, : 2 * COLS]
+            ref[rows, C:] = moved[:, :, 2 * COLS :]
+
     def fanned(values):
         both = dot(jnp.concatenate(split(values), axis=0), one_hot)
         return both[:C] + both[C:]
@@ -231,7 +252,9 @@
         side = side + u_side
         x0[e, :, :COLS] = main
         x0[e, :, COLS:] = side
-        put_shifted(xh, xl, e, main, side, d0, False)
+        for ref, a, b in zip((mh, ml), split(main), split(side)):
+            ref[e, :, :COLS] = a
+            ref[e, :, COLS:] = b
 
     fan_low = fanned(row_u), fanned(turn(row_u, -8))
     fan_high = fanned(turn(row_u, -(HALO + ROWS))), fanned(turn(row_u, -(HALO + ROWS + 8)))
@@ -243,6 +266,7 @@
         assemble(f, f // 8, f % 8, below, fan_high[at // 8][:, part], row_mask(f))
 
     def assemble_own(q, carry):
+        shift_rows(8 * q + 4, 8)
         fan = fanned(turn(row_u, (COLS - HALO - 8 * q) % COLS))
         for s in range(8):
             k, slot = q + 1 + (s + 4) // 8, (s + 4) % 8
@@ -253,15 +277,21 @@
         return carry
 
     lax.fori_loop(0, ROWS // 8, assemble_own, 0)
+    shift_rows(0, 4)
+    shift_rows(HALO + ROWS - 8, HALO + 8)
 
     def stacked(ref, lowest, middle, highest):
         return jnp.concatenate([ref[lowest], ref[middle], ref[highest]], axis=0)
 
     def first(i, carry):
         e = i + 4
-        acc = weighted(
-            wts[0], stacked(xh, e - d0, e, e + d0), stacked(xl, e - d0, e, e + d0)
+        x_hi, x_lo = (
+            jnp.concatenate(
+                [piece for at in (e - d0, e, e + d0) for piece in (ref[at, :C], middle[at], ref[at, C:])], axis=0
+            )
+            for ref, middle in ((xh, mh), (xl, ml))
         )
+        acc = weighted(wts[0], x_hi, x_lo)
         t = jnp.tanh(acc)
         t0s[e] = t[:, :COLS]
         keep = row_mask(e)
@@ -384,8 +414,10 @@
         ],
         scratch_shapes=[
             pltpu.VMEM((EXT, C, 2 * COLS), F32),
-            pltpu.VMEM((EXT, 3 * C, 2 * COLS), BF16),
-            pltpu.VMEM((EXT, 3 * C, 2 * COLS), BF16),
+            pltpu.VMEM((EXT, C, 2 * COLS), BF16),
+            pltpu.VMEM((EXT, C, 2 * COLS), BF16),
+            pltpu.VMEM((EXT, 2 * C, 2 * COLS), BF16),
+            pltpu.VMEM((EXT, 2 * C, 2 * COLS), BF16),
             pltpu.VMEM((EXT, 3 * C, 2 * COLS), BF16),
             pltpu.VMEM((EXT, 3 * C, 2 * COLS), BF16),
             pltpu.VMEM((GEXT, 3 * C, COLS), BF16),
@@ -467,8 +499,10 @@
     col_b = lax.ppermute(strip_b, "col", col_second)
     col_a = lax.ppermute(strip_a, "col", col_first)
 
-    own = jnp.sum(parts, axis=0)
-    fields = jnp.broadcast_to(own, (PEERS,) + own.shape)
+    fields = pl.pallas_call(
+        combine_kernel, in_specs=[VMEM], out_specs=VMEM, out_shape=packs,
+        compiler_params=pltpu.CompilerParams(vmem_limit_bytes=2 * 2**20), name="combine",
+    )(parts)
     fields = lax.all_to_all(fields, "row", 0, 0, tiled=True, axis_index_groups=same_core)
 
     pair_out, send = layers(dilation, pair, cot, row_a, row_b, col_a, col_b, fields, wts)

time: 89.8 us -> 87.9 us (0.979)
  other arithmetic: 0.97 us -> 0.02 us
    reduce_sum x1 -> x0, other arithmetic: 0.95 us -> none  [local(): own = jnp.sum(parts, axis=0)]
where the time goes in v4:
time: 87.9 us; the launch traced here: 87.5 us
  blocking collectives  32.5 us (37%)
  Pallas kernels  22.9 us (26%)
  starting transfers between devices  19.9 us (23%)
  waiting for transfers between devices  11.3 us (13%)
    all_to_all x1, blocking collectives, local(): lax.all_to_all(jnp.broadcast_to(own, (PEERS,) + own.shape), ('row', 'col'...  19.7 us
    pallas_call x1, Pallas kernels, layers(): pl.pallas_call(main_kernel, in_specs=[SMEM] + [VMEM] * 8, out_specs=[pl.B...  14.1 us
    all_to_all x1, blocking collectives, local(): lax.all_to_all(send, 'row', 0, 0, tiled=True, axis_index_groups=same_core)  12.8 us
    all_to_all x1, starting transfers between devices, local(): lax.all_to_all(parts, ('row', 'col'), 0, 0, tiled=True, axis_index_groups...  7 us
    all_to_all x1, starting transfers between devices, local(): lax.all_to_all(fields, 'row', 0, 0, tiled=True, axis_index_groups=same_core)  6.47 us
    all_to_all x1, waiting for transfers between devices, local(): lax.all_to_all(parts, ('row', 'col'), 0, 0, tiled=True, axis_index_groups...  5.07 us
    ppermute x1, waiting for transfers between devices, local(): col_a = lax.ppermute(strip_a, 'col', col_first)  4.5 us
    pallas_call x1, Pallas kernels, local(): pl.pallas_call(strips_kernel, in_specs=[VMEM] * 4, out_specs=[VMEM] * 2,...  4.12 us
  transfers between devices with their start and end apart: 6, of which 3 were waited for; matrix products, arithmetic and copies ran while one was open for 0% of the time, Pallas kernels for 5%

profile of v4, /device:TPU:1, one launch (start us, length us, event | category | flops | bytes accessed | tf_op | source)
XLA Modules:
  0.0 87.5 jit_solution(13674700002372465388)
XLA Ops:
  0.6 0.0 copy-start.2
  0.6 0.0 copy-start.1
  0.6 2.6 %open.1 = (f32[16,24,128]{2,1,0:T(8,128)}, f32[16,48,128]{2,1,0:T(8,128)}, f32[16,48,128]{2,1,0:T(8,128)}) custom-call(f32[32,64]{1,0:T(8,128)} %embed_hbm.1, f32[48,64]{1,0:T(8,128)} %bitcast.14, f32[1536,128]{1,0:T(8,128)} %bitcast.7, f32[1536,128]{1,0:T(8,128)} %bitcast.10), custom_call_target="tpu_custom_call" | custom-call | tf_op jit(solution)/shard_map/open/pallas_call | solution.py:468
  3.3 0.0 copy-start
  3.3 3.3 %collective-permute-start = (f32[16,48,128]{2,1,0:T(8,128)}, f32[16,48,128]{2,1,0:T(8,128)S(1)}, u32[]{:S(2)}, u32[]{:S(2)}) collective-permute-start(f32[16,48,128]{2,1,0:T(8,128)} %get-tuple-element.13), channel_id=1, source_target_pairs={{0,8},{8,0},{16,24},{24,16},{32,40},{40,32},{48,56},{56,48},{64,72... | collective-permute-start | bytes 1179656 | tf_op jit(solution)/shard_map/ppermute | solution.py:480
  6.6 1.9 %collective-permute-start.1 = (f32[16,48,128]{2,1,0:T(8,128)}, f32[16,48,128]{2,1,0:T(8,128)S(1)}, u32[]{:S(2)}, u32[]{:S(2)}) collective-permute-start(f32[16,48,128]{2,1,0:T(8,128)} %get-tuple-element.14), channel_id=1, source_target_pairs={{8,16},{16,8},{24,32},{32,24},{40,48},{48,40},{56,64},{64,56},{72,... | collective-permute-start | bytes 1179656 | tf_op jit(solution)/shard_map/ppermute | solution.py:479
  8.5 7.0 %all-to-all-start = ((f32[16,24,128]{2,1,0:T(8,128)}), f32[16,24,128]{2,1,0:T(8,128)S(1)}, u32[]{:S(2)}, u32[]{:S(2)}) async-start(f32[16,24,128]{2,1,0:T(8,128)} %get-tuple-element.15), calls=%async_computation | async-start | bytes 393216 | tf_op jit(solution)/shard_map/all_to_all | solution.py:482
  15.5 0.0 copy-done.2
  15.5 0.4 weights.1.wts
  15.9 0.0 collective-permute-done.got_a.row_a
  15.9 0.0 collective-permute-done.1.got_b.row_b
  15.9 0.0 copy-done.1
  16.0 0.0 copy-done
  16.0 4.1 %strips.1 = (f32[7,48,128]{2,1,0:T(8,128)}, f32[7,48,128]{2,1,0:T(8,128)S(1)}) custom-call(f32[1536,128]{1,0:T(8,128)S(1)} %bitcast.8, f32[1536,128]{1,0:T(8,128)S(1)} %bitcast.11, f32[16,48,128]{2,1,0:T(8,128)S(1)} %collective-permute-done.got_a.row_a, f32[16,48,128]{2,1,0:T(8,128)S(1)} %collective-permute-done.1.got_b.row_b), custom_call_target="tpu_custom_call" | custom-call | tf_op jit(solution)/shard_map/strips/pallas_call | solution.py:484
  20.1 5.1 %all-to-all-done.parts = f32[16,24,128]{2,1,0:T(8,128)S(1)} async-done(((f32[16,24,128]{2,1,0:T(8,128)}), f32[16,24,128]{2,1,0:T(8,128)S(1)}, u32[]{:S(2)}, u32[]{:S(2)}) %all-to-all-start) | async-done | bytes 196640 | tf_op jit(solution)/shard_map/all_to_all | solution.py:482
  25.2 0.7 combine.1
  25.9 0.0 copy-start.4
  25.9 6.5 %all-to-all-start.1 = ((f32[16,24,128]{2,1,0:T(8,128)}), f32[16,24,128]{2,1,0:T(8,128)S(1)}, u32[]{:S(2)}, u32[]{:S(2)}) async-start(f32[16,24,128]{2,1,0:T(8,128)} %combine.1), calls=%async_computation.1 | async-start | bytes 393216 | tf_op jit(solution)/shard_map/all_to_all | solution.py:506
  32.3 0.4 collective-permute-start.2
  32.7 0.8 collective-permute-start.3
  33.6 4.5 %collective-permute-done.2.col_a = f32[7,48,128]{2,1,0:T(8,128)S(1)} collective-permute-done((f32[7,48,128]{2,1,0:T(8,128)}, f32[7,48,128]{2,1,0:T(8,128)S(1)}, u32[]{:S(2)}, u32[]{:S(2)}) %collective-permute-start.2) | collective-permute-done | bytes 172064 | tf_op jit(solution)/shard_map/ppermute | solution.py:500
  38.1 0.0 collective-permute-done.3.col_b
  38.1 1.8 %all-to-all-done.1.fields = f32[16,24,128]{2,1,0:T(8,128)S(1)} async-done(((f32[16,24,128]{2,1,0:T(8,128)}), f32[16,24,128]{2,1,0:T(8,128)S(1)}, u32[]{:S(2)}, u32[]{:S(2)}) %all-to-all-start.1) | async-done | bytes 196640 | tf_op jit(solution)/shard_map/all_to_all | solution.py:506
  39.8 0.0 copy-done.4
  39.8 14.1 %layers.1 = (f32[1536,128]{1,0:T(8,128)}, f32[16,24,128]{2,1,0:T(8,128)S(1)}) custom-call(s32[2]{0:T(128)S(1)} %copy-done.4, f32[1536,128]{1,0:T(8,128)S(1)} %bitcast.9, f32[1536,128]{1,0:T(8,128)S(1)} %bitcast.12, f32[16,48,128]{2,1,0:T(8,128)S(1)} %collective-permute-done.got_a.row_a, f32[16,48,128]{2,1,0:T(8,128)S(1)} %collective-permute-done.1.got_b.row_b, ...), custom_call_target="tpu_custom_call" | custom-call | tf_op jit(solution)/shard_map/layers/pallas_call | solution.py:407
  53.9 12.8 %all_to_all.20 = f32[16,24,128]{2,1,0:T(8,128)S(1)} all-to-all(f32[16,24,128]{2,1,0:T(8,128)S(1)} %get-tuple-element.23), channel_id=1, replica_groups={{0,16,32,48,64,80,96,112,128,144,160,176,192,208,224,240},{8,24,40,56,7..., dimensions={0} | all-to-all | bytes 393216 | tf_op jit(solution)/shard_map/all_to_all | solution.py:510
  66.8 0.0 copy-start.3
  66.8 19.7 %all_to_all.21.parts = f32[16,24,128]{2,1,0:T(8,128)S(1)} all-to-all(f32[16,24,128]{2,1,0:T(8,128)S(1)} %broadcast_in_dim.3), channel_id=1, replica_groups={{0,1,2,3,4,5,6,7,8,9,10,11,12,13,14,15},{16,17,18,19,20,21,22,23,24,25,..., dimensions={0} | all-to-all | bytes 393216 | tf_op jit(solution)/shard_map/all_to_all | solution.py:512
  86.5 0.0 copy-done.3
  86.5 0.9 %finish.1 = f32[32,64]{1,0:T(8,128)} custom-call(f32[16,24,128]{2,1,0:T(8,128)S(1)} %all_to_all.21.parts, f32[48,64]{1,0:T(8,128)S(1)} %bitcast.15), custom_call_target="tpu_custom_call" | custom-call | tf_op jit(solution)/shard_map/finish/pallas_call | solution.py:515
  (2 shorter events, 0.0 us)
Async XLA Ops:
  0.6 14.9 %copy-start.2 = (f32[2,48,48,3,3]{2,1,4,3,0:T(8,128)S(1)}, f32[2,48,48,3,3]{2,1,4,3,0:T(8,128)}, u32[]{:S(2)}) copy-start(f32[2,48,48,3,3]{2,1,4,3,0:T(8,128)} %param.9) | copy-start | bytes 497668
  0.6 15.3 %copy-start.1 = (f32[48,32,128]{2,1,0:T(8,128)S(1)}, f32[48,32,128]{2,1,0:T(8,128)}, u32[]{:S(2)}) copy-start(f32[48,32,128]{2,1,0:T(8,128)} %param.11) | copy-start | bytes 2359300
  3.3 12.7 %copy-start = (f32[48,32,128]{2,1,0:T(8,128)S(1)}, f32[48,32,128]{2,1,0:T(8,128)}, u32[]{:S(2)}) copy-start(f32[48,32,128]{2,1,0:T(8,128)} %param.8) | copy-start | bytes 2359300
  3.3 12.6 %collective-permute-start = (f32[16,48,128]{2,1,0:T(8,128)}, f32[16,48,128]{2,1,0:T(8,128)S(1)}, u32[]{:S(2)}, u32[]{:S(2)}) collective-permute-start(f32[16,48,128]{2,1,0:T(8,128)} %get-tuple-element.13), channel_id=1, source_target_pairs={{0,8},{8,0},{16,24},{24,16},{32,40},{40,32},{48,56},{56,48},{64,72... | collective-permute-start | bytes 1179656 | tf_op jit(solution)/shard_map/ppermute | solution.py:480
  6.6 9.3 %collective-permute-start.1 = (f32[16,48,128]{2,1,0:T(8,128)}, f32[16,48,128]{2,1,0:T(8,128)S(1)}, u32[]{:S(2)}, u32[]{:S(2)}) collective-permute-start(f32[16,48,128]{2,1,0:T(8,128)} %get-tuple-element.14), channel_id=1, source_target_pairs={{8,16},{16,8},{24,32},{32,24},{40,48},{48,40},{56,64},{64,56},{72,... | collective-permute-start | bytes 1179656 | tf_op jit(solution)/shard_map/ppermute | solution.py:479
  8.5 16.6 %all-to-all-start = ((f32[16,24,128]{2,1,0:T(8,128)}), f32[16,24,128]{2,1,0:T(8,128)S(1)}, u32[]{:S(2)}, u32[]{:S(2)}) async-start(f32[16,24,128]{2,1,0:T(8,128)} %get-tuple-element.15), calls=%async_computation | async-start | bytes 393216 | tf_op jit(solution)/shard_map/all_to_all | solution.py:482
  25.9 14.0 %copy-start.4 = (s32[2]{0:T(128)S(1)}, s32[2]{0:T(128)}, u32[]{:S(2)}) copy-start(s32[2]{0:T(128)} %dil.1) | copy-start | bytes 28
  25.9 14.0 %all-to-all-start.1 = ((f32[16,24,128]{2,1,0:T(8,128)}), f32[16,24,128]{2,1,0:T(8,128)S(1)}, u32[]{:S(2)}, u32[]{:S(2)}) async-start(f32[16,24,128]{2,1,0:T(8,128)} %combine.1), calls=%async_computation.1 | async-start | bytes 393216 | tf_op jit(solution)/shard_map/all_to_all | solution.py:506
  32.3 5.7 %collective-permute-start.2 = (f32[7,48,128]{2,1,0:T(8,128)}, f32[7,48,128]{2,1,0:T(8,128)S(1)}, u32[]{:S(2)}, u32[]{:S(2)}) collective-permute-start(f32[7,48,128]{2,1,0:T(8,128)} %get-tuple-element.18), channel_id=1, source_target_pairs={{0,1},{1,0},{2,3},{3,2},{4,5},{5,4},{6,7},{7,6},{8,9},{9,8},{10,11... | collective-permute-start | bytes 516104 | tf_op jit(solution)/shard_map/ppermute | solution.py:500
  32.7 5.3 %collective-permute-start.3 = (f32[7,48,128]{2,1,0:T(8,128)S(1)}, f32[7,48,128]{2,1,0:T(8,128)S(1)}, u32[]{:S(2)}, u32[]{:S(2)}) collective-permute-start(f32[7,48,128]{2,1,0:T(8,128)S(1)} %get-tuple-element.19), channel_id=1, source_target_pairs={{1,2},{2,1},{3,4},{4,3},{5,6},{6,5},{9,10},{10,9},{11,12},{12,11},... | collective-permute-start | bytes 516104 | tf_op jit(solution)/shard_map/ppermute | solution.py:499
  66.8 19.7 %copy-start.3 = (f32[64,48]{0,1:T(8,128)S(1)}, f32[64,48]{0,1:T(8,128)}, u32[]{:S(2)}) copy-start(f32[64,48]{0,1:T(8,128)} %param.7) | copy-start | bytes 36868
